TPU v7x, 256 devices: a whole 4x4x8 slice. The times are simulated.
256 devices in a mesh: ta: 2 (over x_lo), gx: 128 (over y, x_hi, z, core).
Axes of the slice: x: 4 (x_hi: 2, x_lo: 2; x = x_hi * 2 + x_lo), y: 4, z: 8, core: 2. Of those that a mesh axis runs over, the one named last changes fastest.
Arguments:
- voltages: bfloat16 [1024, 1048576], P('gx', 'ta'), may hold values from -8 to 7, as said below
Outputs:
- visibility: float32 [2, 128, 1024, 1024], P(None, 'gx', 'ta')
Inputs may be any that keep to these rules, and one draw needn't show every extreme that they name: `voltages`: integer values: 4-bit quantized samples, a noise part plus a sky signal common to the inputs with integer gains.
All inputs are finite; a program needn't handle non-finite values.
Results may differ from a plain program's by a relative error of at most 0.00075.
Values may be sent and summed in bfloat16 or wider, within the bound.
No kernel may reach another device: no remote copies, remote signals or barrier semaphores. Data moves between devices by JAX's collectives and lax.ppermute only.
A program may use at most 64 MiB of HBM per device.

v0:
```python
import jax
import jax.numpy as jnp
from jax import lax
from jax.sharding import PartitionSpec as P

FRAME = 2048
TAPS = 4
CH_DEV = 1


def from_behind(block, axis, distance):
    devices = range(lax.axis_size(axis))
    route = [(i - distance, i) for i in devices if i - distance in devices]
    return lax.ppermute(block, axis, route)


def pfb_window():
    length = TAPS * FRAME
    points = jnp.arange(length, dtype=jnp.float32)
    shaped = jnp.sinc((points - length / 2 + 0.5) / FRAME) * (
        0.54 - 0.46 * jnp.cos(2.0 * jnp.pi * points / (length - 1))
    )
    return shaped.reshape(TAPS, FRAME)


def dft_table(count):
    channel = jnp.arange(count, dtype=jnp.int32)[:, None]
    sample = jnp.arange(FRAME, dtype=jnp.int32)[None, :]
    phase = (channel * sample % FRAME).astype(jnp.float32) * (2.0 * jnp.pi / FRAME)
    return jnp.concatenate([jnp.cos(phase), -jnp.sin(phase)], 0)


def filter_frames(padded, span):
    window = pfb_window()
    filtered = window[0][None, None, :] * padded[:, 0:span, :].astype(jnp.float32)
    for tap_index in range(1, TAPS):
        filtered = filtered + window[tap_index][None, None, :] * padded[
            :, tap_index : tap_index + span, :
        ].astype(jnp.float32)
    return filtered


def pair_products(left_real, left_imag, right_real, right_imag):
    vis_real = jnp.einsum(
        "cis,cjs->cij", left_real, right_real, preferred_element_type=jnp.float32
    ) + jnp.einsum("cis,cjs->cij", left_imag, right_imag, preferred_element_type=jnp.float32)
    vis_imag = jnp.einsum(
        "cis,cjs->cij", left_imag, right_real, preferred_element_type=jnp.float32
    ) - jnp.einsum("cis,cjs->cij", left_real, right_imag, preferred_element_type=jnp.float32)
    return jnp.stack([vis_real, vis_imag])


def local(voltages):
    in_dev = voltages.shape[0]
    s_dev = voltages.shape[1] // FRAME
    n_time = lax.axis_size("ta")
    n_chan = CH_DEV * lax.axis_size("gx")
    frames = voltages.reshape(in_dev, s_dev, FRAME)
    earlier = from_behind(frames[:, s_dev - TAPS + 1 :, :], "ta", 1)
    padded = jnp.concatenate([earlier, frames], 1)
    filtered = filter_frames(padded, s_dev)
    spectra = jnp.einsum(
        "isn,cn->cis", filtered, dft_table(n_chan), precision=lax.Precision.HIGHEST
    )
    spectra = spectra.astype(jnp.bfloat16).reshape(2, n_chan, in_dev, s_dev)
    turned = lax.all_to_all(spectra, "gx", split_axis=1, concat_axis=2, tiled=True)
    norm_scale = 1.0 / (16.0 * FRAME * s_dev * n_time)
    gram_sum = pair_products(turned[0], turned[1], turned[0], turned[1]) * norm_scale
    return lax.psum_scatter(gram_sum, "ta", scatter_dimension=2, tiled=True)


def solution(mesh):
    in_specs = (P("gx", "ta"),)
    out_specs = P(None, "gx", "ta", None)
    return jax.shard_map(local, mesh=mesh, in_specs=in_specs, out_specs=out_specs, check_vma=False)
```

profile of v0, /device:TPU:1, one launch (start us, length us, event | category | flops | bytes accessed | tf_op | source)
XLA Modules:
  0.0 218.0 jit_solution(13286923825884728806)
XLA Ops:
  6.5 0.0 reduce-scatter.2.cloned.1.call-start
  6.5 11.2 %copy.9 = bf16[8,256,2048]{2,1,0:T(8,128)(2,1)} copy(bf16[8,256,2048]{2,0,1:T(8,128)(2,1)} %bitcast.25) | data formatting | bytes 16777216 | tf_op jit(solution)/shard_map/reshape | solution.py:58
  17.8 1.0 slice.50
  18.8 4.1 %collective-permute-start = (bf16[8,3,2048]{2,1,0:T(4,128)(2,1)S(1)}, bf16[8,3,2048]{2,1,0:T(4,128)(2,1)S(1)}, u32[]{:S(2)}, u32[]{:S(2)}) collective-permute-start(bf16[8,3,2048]{2,1,0:T(4,128)(2,1)S(1)} %slice.50), channel_id=1, source_target_pairs={{0,128},{1,129},{2,130},{3,131},{4,132},{5,133},{6,134},{7,135},{8... | collective-permute-start | bytes 294920 | tf_op jit(solution)/shard_map/ppermute | solution.py:14
  22.9 0.2 fusion.42
  23.1 4.1 %sine_negate_fusion = (f32[128,2048]{1,0:T(8,128)S(1)}, f32[128,2048]{1,0:T(8,128)S(1)}) fusion(), kind=kLoop, calls=%fused_computation.38 | loop fusion | flops 3932160 | bytes 2097152 | tf_op jit(solution)/shard_map/neg | solution.py:30
  27.2 0.0 collective-permute-done
  27.2 30.8 %fusion.26 = bf16[256,8,256]{2,0,1:T(8,128)(2,1)S(1)} fusion(bf16[8,256,2048]{2,1,0:T(8,128)(2,1)} %copy.9, bf16[8,3,2048]{2,1,0:T(4,128)(2,1)S(1)} %collective-permute-done, f32[2048]{0:T(1024)S(1)} %get-tuple-element.6, f32[2048]{0:T(1024)S(1)} %get-tuple-element.7, f32[2048]{0:T(1024)S(1)} %get-tuple-element.8, f32[2048]{0:T(1024)S(1)} %get-tuple-element.5, ...), kind=kOutput, calls=%fused_computation.34 | convolution fusion | flops 12969836544 | bytes 11665408 | tf_op jit(solution)/shard_map/isn,cn->cis/dot_general | solution.py:62
  58.1 0.6 copy.12
  58.7 47.4 %all_to_all.4 = bf16[2,128,8,256]{3,2,0,1:T(8,128)(2,1)S(1)} all-to-all(bf16[2,128,8,256]{3,2,0,1:T(8,128)(2,1)S(1)} %copy.12), channel_id=1, replica_groups=mesh['ta'=2,'gx'=128] {'gx'}, dimensions={1} | all-to-all | bytes 2097152 | tf_op jit(solution)/shard_map/all_to_all | solution.py:66
  106.0 0.7 fusion.36
  106.8 0.7 fusion.37
  107.5 0.7 subtract_bitcast_fusion
  108.3 0.7 add_bitcast_fusion
  109.0 4.2 %maximum_multiply_fusion = f32[2,1,1024,1024]{3,2,1,0:T(8,128)} fusion(f32[1,1,1024,1024]{3,2,1,0:T(8,128)S(1)} %subtract_bitcast_fusion, f32[1,1,1024,1024]{3,2,1,0:T(8,128)S(1)} %add_bitcast_fusion), kind=kLoop, calls=%fused_computation.21 | loop fusion | flops 4194304 | bytes 16777216 | tf_op jit(solution)/shard_map/mul | solution.py:68
  113.2 0.0 reduce-scatter.2.cloned.1.call-update
  113.3 97.9 %reduce-scatter.2.cloned.1.call-done = f32[2,1,512,1024]{3,2,1,0:T(8,128)} async-done(((f32[2,1,1024,1024]{3,2,1,0:T(8,128)}), f32[2,1,512,1024]{3,2,1,0:T(8,128)}) %reduce-scatter.2.cloned.1.call-update) | async-done | bytes 4194320 | tf_op jit(solution)/shard_map/reduce_scatter | solution.py:69
  (1 shorter events, 0.0 us)
Async XLA Ops:
  6.5 204.6 %reduce-scatter.2.cloned.1.call-start = ((), (), s32[]{:S(2)}) async-start(), calls=%async_computation.2 | async-start | bytes 12582912 | tf_op jit(solution)/shard_map/reduce_scatter | solution.py:69
  18.8 8.4 %collective-permute-start = (bf16[8,3,2048]{2,1,0:T(4,128)(2,1)S(1)}, bf16[8,3,2048]{2,1,0:T(4,128)(2,1)S(1)}, u32[]{:S(2)}, u32[]{:S(2)}) collective-permute-start(bf16[8,3,2048]{2,1,0:T(4,128)(2,1)S(1)} %slice.50), channel_id=1, source_target_pairs={{0,128},{1,129},{2,130},{3,131},{4,132},{5,133},{6,134},{7,135},{8... | collective-permute-start | bytes 294920 | tf_op jit(solution)/shard_map/ppermute | solution.py:14
Sparse Core Ops, SparseCore 0:
  113.4 97.7 reduce-scatter.1
where the time goes:
time: 218 us
  waiting for transfers between devices  97.9 us (45%)
  blocking collectives  47.4 us (22%)
  matrix products  33.8 us (16%)
  between operations  13.5 us (6%)
  local copies, waits for them, and re-layouts  12.8 us (6%)
  other arithmetic  8.48 us (4%)
  starting transfers between devices  4.13 us (2%)
    reduce_scatter x1, waiting for transfers between devices, local(): return lax.psum_scatter(gram_sum, 'ta', scatter_dimension=2, tiled=True)  97.9 us
    all_to_all x1, blocking collectives, local(): lax.all_to_all(spectra, 'gx', split_axis=1, concat_axis=2, tiled=True)  47.4 us
    dot_general x1, matrix products, local(): jnp.einsum('isn,cn->cis', filtered, dft_table(n_chan), precision=lax.Prec...  30.8 us
    reshape x1, local copies, waits for them, and re-layouts, local(): frames = voltages.reshape(in_dev, s_dev, FRAME)  11.2 us
  transfers between devices with their start and end apart: 2, of which 1 were waited for; matrix products, arithmetic and copies ran while one was open for 2% of the time, Pallas kernels for 0%

commit v1 on v0

v1 whole, which is shorter than its diff:
```python
import functools

import jax
import jax.numpy as jnp
import ml_dtypes
import numpy as np
from jax import lax
from jax.experimental import pallas as pl
from jax.experimental.pallas import tpu as pltpu
from jax.sharding import PartitionSpec as P

FRAME = 2048
TAPS = 4
BLOCK = 128
HALO = 4
VMEM = 56 * 1024 * 1024


def folded_table(count):
    length = TAPS * FRAME
    points = np.arange(length, dtype=np.float64)
    window = np.sinc((points - length / 2 + 0.5) / FRAME) * (
        0.54 - 0.46 * np.cos(2.0 * np.pi * points / (length - 1))
    )
    window = window.reshape(TAPS, FRAME)
    phase = (np.arange(FRAME)[:, None] * np.arange(count)[None, :] % FRAME) * (
        2.0 * np.pi / FRAME
    )
    dft = np.concatenate([np.cos(phase), -np.sin(phase)], 1)
    return (window[:, :, None] * dft[None]).astype(ml_dtypes.bfloat16)


def filterbank_kernel(frames, halo, table, out, rows, summed, turned):
    tap = pl.program_id(1)
    inputs = frames.shape[1]
    count = out.shape[0]
    span = BLOCK * inputs

    @pl.when(tap == 0)
    def _():
        rows[0 : HALO * inputs, :] = (
            halo[0].astype(jnp.float32).reshape(HALO * inputs, FRAME).astype(jnp.bfloat16)
        )

        def pack(step, carry):
            some = frames[pl.ds(step * 4, 4)].astype(jnp.float32)
            at = pl.multiple_of(HALO * inputs + step * 4 * inputs, 16)
            rows[pl.ds(at, 4 * inputs), :] = some.reshape(4 * inputs, FRAME).astype(jnp.bfloat16)
            return carry

        lax.fori_loop(0, BLOCK // 4, pack, 0)

    product = jnp.dot(rows[...], table[0], preferred_element_type=jnp.float32)

    for k in range(TAPS):

        @pl.when(tap == k)
        def _():
            start = (k + HALO - TAPS + 1) * inputs
            term = product[start : start + span]
            for part in range(2):
                half = term[:, part * count : (part + 1) * count]
                if k == 0:
                    summed[part] = half
                else:
                    summed[part] += half

    @pl.when(tap == TAPS - 1)
    def _():
        for part in range(2):
            for i in range(inputs):
                one = summed[part, pl.ds(i, BLOCK, stride=inputs), :]
                turned[pl.ds(part * inputs + i, count, stride=2 * inputs), :] = one.T
        out[...] = turned[...].reshape(count, 2 * inputs, BLOCK).astype(jnp.bfloat16)


def filterbank(frames, halo, table):
    spectra, inputs, _ = frames.shape
    count = table.shape[2] // 2
    blocks = spectra // BLOCK
    return pl.pallas_call(
        filterbank_kernel,
        grid=(blocks, TAPS),
        in_specs=[
            pl.BlockSpec((BLOCK, inputs, FRAME), lambda b, k: (b, 0, 0)),
            pl.BlockSpec((1, HALO, inputs, FRAME), lambda b, k: (b, 0, 0, 0)),
            pl.BlockSpec((1, FRAME, 2 * count), lambda b, k: (k, 0, 0)),
        ],
        out_specs=pl.BlockSpec((count, 2 * inputs, BLOCK), lambda b, k: (0, 0, b)),
        out_shape=jax.ShapeDtypeStruct((count, 2 * inputs, spectra), jnp.bfloat16),
        scratch_shapes=[
            pltpu.VMEM(((HALO + BLOCK) * inputs, FRAME), jnp.bfloat16),
            pltpu.VMEM((2, BLOCK * inputs, count), jnp.float32),
            pltpu.VMEM((2 * inputs * count, BLOCK), jnp.float32),
        ],
        compiler_params=pltpu.CompilerParams(vmem_limit_bytes=VMEM),
    )(frames, halo, table)


def visibility_kernel(scale, row_tile, where, mine, other, out, left, right):
    step = pl.program_id(0)
    groups, both, span = mine.shape
    per = both // 2
    total = groups * per

    @pl.when(step == 0)
    def _():
        for t, source in enumerate((mine, other)):
            wide = source[...].astype(jnp.float32).reshape(groups, 2, per, span)
            real = wide[:, 0].reshape(total, span)
            imag = wide[:, 1].reshape(total, span)
            at, far = t * span, (2 + t) * span
            right[:, at : at + span] = real.astype(jnp.bfloat16)
            right[:, far : far + span] = imag.astype(jnp.bfloat16)
            left[:, at : at + span] = imag.astype(jnp.bfloat16)
            left[:, far : far + span] = (-real).astype(jnp.bfloat16)

    first = pl.multiple_of(where[0] + step * row_tile, row_tile)
    dims = (((1,), (1,)), ((), ()))
    out[0, 0] = (
        lax.dot_general(
            right[pl.ds(first, row_tile), :], right[...], dims, preferred_element_type=jnp.float32
        )
        * scale
    )
    out[1, 0] = (
        lax.dot_general(
            left[pl.ds(first, row_tile), :], right[...], dims, preferred_element_type=jnp.float32
        )
        * scale
    )


def visibilities(mine, other, first_row, n_rows, scale):
    groups, both, span = mine.shape
    total = groups * both // 2
    row_tile = 128
    whole = pl.BlockSpec((groups, both, span), lambda r, w: (0, 0, 0))
    return pl.pallas_call(
        functools.partial(visibility_kernel, scale, row_tile),
        grid_spec=pltpu.PrefetchScalarGridSpec(
            num_scalar_prefetch=1,
            grid=(n_rows // row_tile,),
            in_specs=[whole, whole],
            out_specs=pl.BlockSpec((2, 1, row_tile, total), lambda r, w: (0, 0, r, 0)),
            scratch_shapes=[
                pltpu.VMEM((total, 4 * span), jnp.bfloat16),
                pltpu.VMEM((total, 4 * span), jnp.bfloat16),
            ],
        ),
        out_shape=jax.ShapeDtypeStruct((2, 1, n_rows, total), jnp.float32),
        compiler_params=pltpu.CompilerParams(vmem_limit_bytes=VMEM),
    )(first_row, mine, other)


def local(voltages):
    inputs = voltages.shape[0]
    spectra = voltages.shape[1] // FRAME
    n_time = lax.axis_size("ta")
    n_chan = lax.axis_size("gx")
    table = jnp.asarray(folded_table(n_chan))
    frames = voltages.reshape(inputs, spectra, FRAME).transpose(1, 0, 2)
    last = voltages[:, (spectra - HALO) * FRAME :]
    earlier = lax.ppermute(last, "ta", [(i, i + 1) for i in range(n_time - 1)])
    inner = [voltages[:, (b * BLOCK - HALO) * FRAME : b * BLOCK * FRAME] for b in range(1, spectra // BLOCK)]
    halo = jnp.stack([h.reshape(inputs, HALO, FRAME).transpose(1, 0, 2) for h in [earlier, *inner]])
    spectrum = filterbank(frames, halo, table)
    turned = lax.all_to_all(spectrum, "gx", split_axis=0, concat_axis=0, tiled=True)
    other = lax.ppermute(turned, "ta", [(i, (i + 1) % n_time) for i in range(n_time)])
    n_inputs = inputs * n_chan
    n_rows = n_inputs // n_time
    first_row = (lax.axis_index("ta") * n_rows).astype(jnp.int32).reshape(1)
    scale = 1.0 / (16.0 * FRAME * spectra * n_time)
    return visibilities(turned, other, first_row, n_rows, scale)


def solution(mesh):
    in_specs = (P("gx", "ta"),)
    out_specs = P(None, "gx", "ta", None)
    return jax.shard_map(local, mesh=mesh, in_specs=in_specs, out_specs=out_specs, check_vma=False)
```

time: 218 us -> 108 us (0.50)
  waiting for transfers between devices: 97.9 us -> 25.9 us
  matrix products: 33.8 us -> 0 us
  Pallas kernels: 0 us -> 26 us
  between operations: 13.5 us -> 0.02 us
  local copies, waits for them, and re-layouts: 12.8 us -> 2 us
  other arithmetic: 8.48 us -> 0.72 us
    reduce_scatter x1 -> x0, waiting for transfers between devices: 97.9 us -> none  [local(): return lax.psum_scatter(gram_sum, 'ta', scatter_dimension=2, tiled=True)]
    dot_general x5 -> x0, matrix products: 33.8 us -> none  [the longest x1 30.8 us: local(): jnp.einsum('isn,cn->cis', filtered, dft_table(n_chan), precision=lax.Prec...]
    pallas_call x0 -> x2, Pallas kernels: none -> 26 us  [the longest x1 17 us: filterbank(): pl.pallas_call(filterbank_kernel, grid=(blocks, TAPS), in_specs=[pl.Block...]
    ppermute x1 -> x2, waiting for transfers between devices: 0.01 us -> 25.9 us  [the longest x1 23.7 us: local(): lax.ppermute(turned, 'ta', [(i, (i + 1) % n_time) for i in range(n_time)])]
    reshape x2 -> x0, local copies, waits for them, and re-layouts: 11.8 us -> none  [the longest x1 11.2 us: local(): frames = voltages.reshape(in_dev, s_dev, FRAME)]
    mul x2 -> x0, other arithmetic: 4.38 us -> none  [the longest x1 4.21 us: local(): pair_products(turned[0], turned[1], turned[0], turned[1]) * norm_scale]
    neg x1 -> x0, other arithmetic: 4.1 us -> none  [dft_table(): return jnp.concatenate([jnp.cos(phase), -jnp.sin(phase)], 0)]
    ppermute x1 -> x2, starting transfers between devices: 4.13 us -> 5.55 us  [the longest x1 3.95 us: local(): earlier = lax.ppermute(last, 'ta', [(i, i + 1) for i in range(n_time - 1)])]
  transfers between devices with their start and end apart: 2 -> 2, of which waited for: 1 -> 2; matrix products, arithmetic and copies ran while one was open for 2% -> 0% of each run, Pallas kernels for 0% -> 0%
where the time goes in v1:
time: 108 us
  blocking collectives  47.9 us (44%)
  Pallas kernels  26 us (24%)
  waiting for transfers between devices  25.9 us (24%)
  starting transfers between devices  5.55 us (5%)
  local copies, waits for them, and re-layouts  2 us (2%)
    all_to_all x1, blocking collectives, local(): lax.all_to_all(spectrum, 'gx', split_axis=0, concat_axis=0, tiled=True)  47.9 us
    ppermute x1, waiting for transfers between devices, local(): lax.ppermute(turned, 'ta', [(i, (i + 1) % n_time) for i in range(n_time)])  23.7 us
    pallas_call x1, Pallas kernels, filterbank(): pl.pallas_call(filterbank_kernel, grid=(blocks, TAPS), in_specs=[pl.Block...  17 us
    pallas_call x1, Pallas kernels, visibilities(): pl.pallas_call(functools.partial(visibility_kernel, scale, row_tile), gri...  8.97 us
    ppermute x1, starting transfers between devices, local(): earlier = lax.ppermute(last, 'ta', [(i, i + 1) for i in range(n_time - 1)])  3.95 us
  transfers between devices with their start and end apart: 2, of which 2 were waited for; matrix products, arithmetic and copies ran while one was open for 0% of the time, Pallas kernels for 0%

profile of v1, /device:TPU:1, one launch (start us, length us, event | category | flops | bytes accessed | tf_op | source)
XLA Modules:
  0.0 108.1 jit_solution(6122475577228069819)
XLA Ops:
  0.0 1.0 fusion
  1.0 4.0 %collective-permute-start = (bf16[8,8192]{1,0:T(8,128)(2,1)S(1)}, bf16[8,8192]{1,0:T(8,128)(2,1)S(1)}, u32[]{:S(2)}, u32[]{:S(2)}) collective-permute-start(bf16[8,8192]{1,0:T(8,128)(2,1)S(1)} %get-tuple-element.5), channel_id=1, source_target_pairs={{0,128},{1,129},{2,130},{3,131},{4,132},{5,133},{6,134},{7,135},{8... | collective-permute-start | bytes 393224 | tf_op jit(solution)/shard_map/ppermute | solution.py:164
  4.9 2.1 %collective-permute-done = bf16[8,8192]{1,0:T(8,128)(2,1)S(1)} collective-permute-done((bf16[8,8192]{1,0:T(8,128)(2,1)S(1)}, bf16[8,8192]{1,0:T(8,128)(2,1)S(1)}, u32[]{:S(2)}, u32[]{:S(2)}) %collective-permute-start) | collective-permute-done | bytes 131104 | tf_op jit(solution)/shard_map/ppermute | solution.py:164
  7.1 0.7 pad_maximum_fusion.halo
  7.8 17.0 %shard_map.28 = bf16[128,16,256]{2,1,0:T(8,128)(2,1)} custom-call(bf16[256,8,2048]{2,1,0:T(8,128)(2,1)} %bitcast.14, bf16[2,4,8,2048]{3,2,1,0:T(8,128)(2,1)} %pad_maximum_fusion.halo, bf16[4,2048,256]{2,1,0:T(8,128)(2,1)} %constant.10.clone.table), custom_call_target="tpu_custom_call" | custom-call | tf_op jit(solution)/shard_map/pallas_call | solution.py:81
  24.9 47.9 %all_to_all.5.mine = bf16[128,16,256]{2,1,0:T(8,128)(2,1)S(1)} all-to-all(bf16[128,16,256]{2,1,0:T(8,128)(2,1)} %shard_map.28), channel_id=1, replica_groups=mesh['ta'=2,'gx'=128] {'gx'}, dimensions={0} | all-to-all | bytes 2097152 | tf_op jit(solution)/shard_map/all_to_all | solution.py:168
  72.8 0.0 copy-start
  72.8 1.6 %collective-permute-start.1 = (bf16[128,16,256]{2,1,0:T(8,128)(2,1)S(1)}, bf16[128,16,256]{2,1,0:T(8,128)(2,1)S(1)}, u32[]{:S(2)}, u32[]{:S(2)}) collective-permute-start(bf16[128,16,256]{2,1,0:T(8,128)(2,1)S(1)} %all_to_all.5.mine), channel_id=1, source_target_pairs={{0,128},{128,0},{1,129},{129,1},{2,130},{130,2},{3,131},{131,3},{4... | collective-permute-start | bytes 3145736 | tf_op jit(solution)/shard_map/ppermute | solution.py:169
  74.4 23.7 %collective-permute-done.1.other = bf16[128,16,256]{2,1,0:T(8,128)(2,1)S(1)} collective-permute-done((bf16[128,16,256]{2,1,0:T(8,128)(2,1)S(1)}, bf16[128,16,256]{2,1,0:T(8,128)(2,1)S(1)}, u32[]{:S(2)}, u32[]{:S(2)}) %collective-permute-start.1) | collective-permute-done | bytes 1048608 | tf_op jit(solution)/shard_map/ppermute | solution.py:169
  98.1 0.0 copy-start.1
  98.1 0.0 copy-done
  98.1 1.0 copy-done.1
  99.1 9.0 %shard_map.29 = f32[2,1,512,1024]{3,2,1,0:T(8,128)} custom-call(s32[1]{0:T(128)} %bitcast.where, bf16[128,16,256]{2,1,0:T(8,128)(2,1)} %copy-done, bf16[128,16,256]{2,1,0:T(8,128)(2,1)} %copy-done.1), custom_call_target="tpu_custom_call" | custom-call | tf_op jit(solution)/shard_map/pallas_call | solution.py:139
Async XLA Ops:
  1.0 6.1 %collective-permute-start = (bf16[8,8192]{1,0:T(8,128)(2,1)S(1)}, bf16[8,8192]{1,0:T(8,128)(2,1)S(1)}, u32[]{:S(2)}, u32[]{:S(2)}) collective-permute-start(bf16[8,8192]{1,0:T(8,128)(2,1)S(1)} %get-tuple-element.5), channel_id=1, source_target_pairs={{0,128},{1,129},{2,130},{3,131},{4,132},{5,133},{6,134},{7,135},{8... | collective-permute-start | bytes 393224 | tf_op jit(solution)/shard_map/ppermute | solution.py:164
  72.8 25.3 %copy-start = (bf16[128,16,256]{2,1,0:T(8,128)(2,1)}, bf16[128,16,256]{2,1,0:T(8,128)(2,1)S(1)}, u32[]{:S(2)}) copy-start(bf16[128,16,256]{2,1,0:T(8,128)(2,1)S(1)} %all_to_all.5.mine) | copy-start | bytes 3145732
  72.8 25.3 %collective-permute-start.1 = (bf16[128,16,256]{2,1,0:T(8,128)(2,1)S(1)}, bf16[128,16,256]{2,1,0:T(8,128)(2,1)S(1)}, u32[]{:S(2)}, u32[]{:S(2)}) collective-permute-start(bf16[128,16,256]{2,1,0:T(8,128)(2,1)S(1)} %all_to_all.5.mine), channel_id=1, source_target_pairs={{0,128},{128,0},{1,129},{129,1},{2,130},{130,2},{3,131},{131,3},{4... | collective-permute-start | bytes 3145736 | tf_op jit(solution)/shard_map/ppermute | solution.py:169
  98.1 1.0 copy-start.1

commit v2 on v1

v2 whole, which is shorter than its diff:
```python
import functools

import jax
import jax.numpy as jnp
import ml_dtypes
import numpy as np
from jax import lax
from jax.experimental import pallas as pl
from jax.experimental.pallas import tpu as pltpu
from jax.sharding import Mesh
from jax.sharding import PartitionSpec as P

FRAME = 2048
TAPS = 4
BLOCK = 128
HALO = 4
COLUMNS = 256
VMEM = 56 * 1024 * 1024
VMEM_VIS = 28 * 1024 * 1024
PLANE = ("y", "z", "core")
MIB = 1024 * 1024


def folded_table(order):
    length = TAPS * FRAME
    points = np.arange(length, dtype=np.float64)
    window = np.sinc((points - length / 2 + 0.5) / FRAME) * (
        0.54 - 0.46 * np.cos(2.0 * np.pi * points / (length - 1))
    )
    window = window.reshape(TAPS, FRAME)
    phase = (np.arange(FRAME)[:, None] * order[None, :] % FRAME) * (2.0 * np.pi / FRAME)
    dft = np.concatenate([np.cos(phase), -np.sin(phase)], 1)
    return (window[:, :, None] * dft[None]).astype(ml_dtypes.bfloat16)


def filterbank_kernel(frames, halo, table, out, rows, summed, turned):
    tap = pl.program_id(0)
    inputs = frames.shape[1]
    count = out.shape[0]
    span = BLOCK * inputs

    @pl.when(tap == 0)
    def _():
        rows[0 : HALO * inputs, :] = (
            halo[...].astype(jnp.float32).reshape(HALO * inputs, FRAME).astype(jnp.bfloat16)
        )

        def pack(step, carry):
            some = frames[pl.ds(step * 4, 4)].astype(jnp.float32)
            at = pl.multiple_of(HALO * inputs + step * 4 * inputs, 16)
            rows[pl.ds(at, 4 * inputs), :] = some.reshape(4 * inputs, FRAME).astype(jnp.bfloat16)
            return carry

        lax.fori_loop(0, BLOCK // 4, pack, 0)

    product = jnp.dot(rows[...], table[0], preferred_element_type=jnp.float32)

    for k in range(TAPS):

        @pl.when(tap == k)
        def _():
            start = (k + HALO - TAPS + 1) * inputs
            term = product[start : start + span]
            for part in range(2):
                half = term[:, part * count : (part + 1) * count]
                if k == 0:
                    summed[part] = half
                else:
                    summed[part] += half

    @pl.when(tap == TAPS - 1)
    def _():
        for part in range(2):
            for i in range(inputs):
                one = summed[part, pl.ds(i, BLOCK, stride=inputs), :]
                turned[pl.ds(part * inputs + i, count, stride=2 * inputs), :] = one.T
        out[...] = turned[...].reshape(count, 2 * inputs, BLOCK).astype(jnp.bfloat16)


def filterbank(frames, block, halo, halo_block, table):
    _, inputs, _ = frames.shape
    count = table.shape[2] // 2
    return pl.pallas_call(
        filterbank_kernel,
        grid=(TAPS,),
        in_specs=[
            pl.BlockSpec((BLOCK, inputs, FRAME), lambda k: (block, 0, 0)),
            pl.BlockSpec((HALO, inputs, FRAME), lambda k: (halo_block, 0, 0)),
            pl.BlockSpec((1, FRAME, 2 * count), lambda k: (k, 0, 0)),
        ],
        out_specs=pl.BlockSpec((count, 2 * inputs, BLOCK), lambda k: (0, 0, 0)),
        out_shape=jax.ShapeDtypeStruct((count, 2 * inputs, BLOCK), jnp.bfloat16),
        scratch_shapes=[
            pltpu.VMEM(((HALO + BLOCK) * inputs, FRAME), jnp.bfloat16),
            pltpu.VMEM((2, BLOCK * inputs, count), jnp.float32),
            pltpu.VMEM((2 * inputs * count, BLOCK), jnp.float32),
        ],
        compiler_params=pltpu.CompilerParams(vmem_limit_bytes=VMEM),
        cost_estimate=pl.CostEstimate(
            flops=2 * BLOCK * inputs * FRAME * TAPS * 2 * count,
            bytes_accessed=9 * MIB,
            transcendentals=0,
        ),
    )(frames, halo, table)


def visibility_kernel(scale, half, where, *refs):
    sources, (out, right, left) = refs[:-3], refs[-3:]
    step = pl.program_id(0)
    x_hi, first_row = where[0], where[1]
    groups, both, span = sources[0].shape
    per = both // 2
    rows = half * 2
    n_y = 4
    stripe = groups // n_y * per
    n_rows = left.shape[0] // 2
    depth = right.shape[1] // 2

    @pl.when(step == 0)
    def _():
        for at, source in enumerate(sources):
            segment, far_x = at // 2, at % 2
            from_x = (x_hi + far_x) % 2
            for y in range(n_y):
                some = source[y * (groups // n_y) : (y + 1) * (groups // n_y)]
                wide = some.astype(jnp.float32).reshape(groups // n_y, 2, per, span)
                row = pl.multiple_of((y * 2 + from_x) * stripe, stripe)
                for part in range(2):
                    column = part * depth + segment * span
                    right[pl.ds(row, stripe), column : column + span] = (
                        wide[:, part].reshape(stripe, span).astype(jnp.bfloat16)
                    )
        own = right[pl.ds(pl.multiple_of(first_row, n_rows), n_rows), :]
        left[0:n_rows, :] = own
        left[n_rows:, 0:depth] = own[:, depth:]
        left[n_rows:, depth:] = -own[:, 0:depth]

    at = pl.multiple_of(step * COLUMNS, COLUMNS)
    product = lax.dot_general(
        left[...],
        right[pl.ds(at, COLUMNS), :],
        (((1,), (1,)), ((), ())),
        preferred_element_type=jnp.float32,
    )
    out[0, 0] = product[0:n_rows] * scale
    out[1, 0] = product[n_rows:] * scale


def visibilities(sources, where, n_rows, scale):
    groups, both, span = sources[0].shape
    total = groups * both
    depth = span * len(sources) // 2
    whole = pl.BlockSpec((groups, both, span), lambda r, w: (0, 0, 0))
    return pl.pallas_call(
        functools.partial(visibility_kernel, scale, total // 2),
        grid_spec=pltpu.PrefetchScalarGridSpec(
            num_scalar_prefetch=1,
            grid=(total // COLUMNS,),
            in_specs=[whole] * len(sources),
            out_specs=pl.BlockSpec((2, 1, n_rows, COLUMNS), lambda r, w: (0, 0, 0, r)),
            scratch_shapes=[
                pltpu.VMEM((total, 2 * depth), jnp.bfloat16),
                pltpu.VMEM((2 * n_rows, 2 * depth), jnp.bfloat16),
            ],
        ),
        out_shape=jax.ShapeDtypeStruct((2, 1, n_rows, total), jnp.float32),
        compiler_params=pltpu.CompilerParams(vmem_limit_bytes=VMEM_VIS),
    )(where, *sources)


def corner_turn(spectrum):
    count, both, span = spectrum.shape
    plane = spectrum.reshape(count // 2, 2, both, span)
    return lax.all_to_all(plane, PLANE, split_axis=0, concat_axis=0, tiled=True)


def along_x(turned):
    x_hi = lax.axis_index("xh")
    mine = lax.dynamic_index_in_dim(turned, x_hi, 1, keepdims=False)
    theirs = lax.dynamic_index_in_dim(turned, 1 - x_hi, 1, keepdims=False)

    def swap(array, far_x, far_t):
        route = [
            (t * 2 + x, (t ^ far_t) * 2 + (x ^ far_x)) for t in range(2) for x in range(2)
        ]
        return lax.ppermute(array, ("ta", "xh"), route)

    both = swap(theirs, 1, 1)
    far = swap(theirs, 1, 0)
    near = swap(mine, 0, 1)
    return [mine, far, near, both]


def local(voltages):
    inputs = voltages.shape[0]
    spectra = voltages.shape[1] // FRAME
    n_time = lax.axis_size("ta")
    n_y, n_z = lax.axis_size("y"), lax.axis_size("z")
    n_chan = n_y * 2 * n_z * 2
    order = np.arange(n_chan).reshape(n_y, 2, n_z, 2).transpose(0, 2, 3, 1).reshape(-1)
    table = jnp.asarray(folded_table(order))
    frames = voltages.reshape(inputs, spectra, FRAME).transpose(1, 0, 2)

    earlier = lax.ppermute(frames[spectra - HALO :], "ta", [(i, i + 1) for i in range(n_time - 1)])
    late = filterbank(frames, 1, frames, BLOCK // HALO - 1, table)
    late, earlier = lax.optimization_barrier((late, earlier))
    turned_late = corner_turn(late)
    early = filterbank(frames, 0, earlier, 0, table)
    sources_late = along_x(turned_late)
    turned_early = corner_turn(early)
    turned_early, *sources_late = lax.optimization_barrier((turned_early, *sources_late))
    sources_early = along_x(turned_early)

    n_rows = inputs * n_chan // n_time
    where = jnp.stack([lax.axis_index("xh"), lax.axis_index("ta") * n_rows]).astype(jnp.int32)
    scale = 1.0 / (16.0 * FRAME * spectra * n_time)
    return visibilities(sources_late + sources_early, where, n_rows, scale)


def solution(mesh):
    fine = Mesh(mesh.devices.reshape(2, 4, 2, 8, 2), ("ta", "y", "xh", "z", "core"))
    gx = ("y", "xh", "z", "core")
    return jax.shard_map(
        local, mesh=fine, in_specs=(P(gx, "ta"),), out_specs=P(None, gx, "ta", None), check_vma=False
    )
```

time: 108 us -> 88.9 us (0.82)
  blocking collectives: 47.9 us -> 0 us
  starting transfers between devices: 5.55 us -> 29.5 us
  waiting for transfers between devices: 25.9 us -> 32.9 us
    all_to_all x1 -> x0, blocking collectives: 47.9 us -> none  [local(): lax.all_to_all(spectrum, 'gx', split_axis=0, concat_axis=0, tiled=True)]
    all_to_all x0 -> x2, waiting for transfers between devices: none -> 21.5 us  [corner_turn(): return lax.all_to_all(plane, PLANE, split_axis=0, concat_axis=0, tiled=True)]
    all_to_all x0 -> x2, starting transfers between devices: none -> 18.9 us  [corner_turn(): return lax.all_to_all(plane, PLANE, split_axis=0, concat_axis=0, tiled=True)]
    ppermute x2 -> x7, waiting for transfers between devices: 25.9 us -> 11.4 us  [the longest x6 11.4 us: swap(): return lax.ppermute(array, ('ta', 'xh'), route)]
    ppermute x2 -> x7, starting transfers between devices: 5.55 us -> 10.6 us  [the longest x6 6.68 us: swap(): return lax.ppermute(array, ('ta', 'xh'), route)]
    pallas_call x2 -> x3, Pallas kernels: 26 us -> 25 us  [the longest x2 19.6 us: filterbank(): pl.pallas_call(filterbank_kernel, grid=(TAPS,), in_specs=[pl.BlockSpec((B...]
  transfers between devices with their start and end apart: 2 -> 9, of which waited for: 2 -> 4; matrix products, arithmetic and copies ran while one was open for 0% -> 0% of each run, Pallas kernels for 0% -> 22%
where the time goes in v2:
time: 88.9 us; the launch traced here: 88.6 us
  waiting for transfers between devices  32.9 us (37%)
  starting transfers between devices  29.5 us (33%)
  Pallas kernels  25 us (28%)
  local copies, waits for them, and re-layouts  1 us (1%)
    all_to_all x2, waiting for transfers between devices, corner_turn(): return lax.all_to_all(plane, PLANE, split_axis=0, concat_axis=0, tiled=True)  21.5 us
    pallas_call x2, Pallas kernels, filterbank(): pl.pallas_call(filterbank_kernel, grid=(TAPS,), in_specs=[pl.BlockSpec((B...  19.6 us
    all_to_all x2, starting transfers between devices, corner_turn(): return lax.all_to_all(plane, PLANE, split_axis=0, concat_axis=0, tiled=True)  18.9 us
    ppermute x6, waiting for transfers between devices, swap(): return lax.ppermute(array, ('ta', 'xh'), route)  11.4 us
    ppermute x6, starting transfers between devices, swap(): return lax.ppermute(array, ('ta', 'xh'), route)  6.68 us
    pallas_call x1, Pallas kernels, visibilities(): pl.pallas_call(functools.partial(visibility_kernel, scale, total // 2), g...  5.45 us
    ppermute x1, starting transfers between devices, local(): lax.ppermute(frames[spectra - HALO:], 'ta', [(i, i + 1) for i in range(n_...  3.95 us
  transfers between devices with their start and end apart: 9, of which 4 were waited for; matrix products, arithmetic and copies ran while one was open for 0% of the time, Pallas kernels for 22%

profile of v2, /device:TPU:1, one launch (start us, length us, event | category | flops | bytes accessed | tf_op | source)
XLA Modules:
  0.0 88.6 jit_solution(3436484083746027376)
XLA Ops:
  0.0 0.9 %slice.4 = bf16[4,8,2048]{2,1,0:T(8,128)(2,1)S(1)} slice(bf16[256,8,2048]{2,1,0:T(8,128)(2,1)} %bitcast.15), slice={[252:256], [0:8], [0:2048]} | slice | bytes 262144 | tf_op jit(solution)/shard_map/slice | solution.py:204
  0.9 4.0 %collective-permute-start = (bf16[4,8,2048]{2,1,0:T(8,128)(2,1)S(1)}, bf16[4,8,2048]{2,1,0:T(8,128)(2,1)S(1)}, u32[]{:S(2)}, u32[]{:S(2)}) collective-permute-start(bf16[4,8,2048]{2,1,0:T(8,128)(2,1)S(1)} %slice.4), channel_id=1, source_target_pairs={{0,128},{1,129},{2,130},{3,131},{4,132},{5,133},{6,134},{7,135},{8... | collective-permute-start | bytes 393224 | tf_op jit(solution)/shard_map/ppermute | solution.py:204
  4.9 9.8 %shard_map.28 = bf16[128,16,128]{2,1,0:T(8,128)(2,1)} custom-call(bf16[256,8,2048]{2,1,0:T(8,128)(2,1)} %bitcast.16, bf16[256,8,2048]{2,1,0:T(8,128)(2,1)} %bitcast.17, bf16[4,2048,256]{2,1,0:T(8,128)(2,1)} %constant.30.clone.table), custom_call_target="tpu_custom_call" | custom-call | flops 4294967296 | bytes 9437184 | tf_op jit(solution)/shard_map/pallas_call | solution.py:83
  14.7 0.0 collective-permute-done.halo
  14.7 12.6 %all-to-all-start.1 = ((bf16[64,2,16,128]{3,2,1,0:T(8,128)(2,1)}), bf16[64,2,16,128]{3,2,1,0:T(8,128)(2,1)S(1)}, u32[]{:S(2)}, u32[]{:S(2)}) async-start(bf16[64,2,16,128]{3,2,1,0:T(8,128)(2,1)} %bitcast.19), calls=%async_computation.1 | async-start | bytes 1048576 | tf_op jit(solution)/shard_map/all_to_all | solution.py:174
  27.3 0.0 copy-done
  27.3 9.8 %shard_map.29 = bf16[128,16,128]{2,1,0:T(8,128)(2,1)} custom-call(bf16[256,8,2048]{2,1,0:T(8,128)(2,1)} %bitcast.18, bf16[4,8,2048]{2,1,0:T(8,128)(2,1)} %copy-done, bf16[4,2048,256]{2,1,0:T(8,128)(2,1)} %constant.30.clone.table), custom_call_target="tpu_custom_call" | custom-call | flops 4294967296 | bytes 9437184 | tf_op jit(solution)/shard_map/pallas_call | solution.py:83
  37.1 7.5 %all-to-all-done.1 = bf16[64,2,16,128]{3,2,1,0:T(8,128)(2,1)S(1)} async-done(((bf16[64,2,16,128]{3,2,1,0:T(8,128)(2,1)}), bf16[64,2,16,128]{3,2,1,0:T(8,128)(2,1)S(1)}, u32[]{:S(2)}, u32[]{:S(2)}) %all-to-all-start.1) | async-done | bytes 524320 | tf_op jit(solution)/shard_map/all_to_all | solution.py:174
  44.6 6.3 %all-to-all-start = ((bf16[64,2,16,128]{3,2,1,0:T(8,128)(2,1)}), bf16[64,2,16,128]{3,2,1,0:T(8,128)(2,1)S(1)}, u32[]{:S(2)}, u32[]{:S(2)}) async-start(bf16[64,2,16,128]{3,2,1,0:T(8,128)(2,1)} %bitcast.20), calls=%async_computation | async-start | bytes 1048576 | tf_op jit(solution)/shard_map/all_to_all | solution.py:174
  51.0 0.5 collective-permute-start.3
  51.4 2.2 %collective-permute-start.1 = (bf16[64,16,128]{2,1,0:T(8,128)(2,1)S(1)}, bf16[64,16,128]{2,1,0:T(8,128)(2,1)S(1)}, u32[]{:S(2)}, u32[]{:S(2)}) collective-permute-start(bf16[64,16,128]{2,1,0:T(8,128)(2,1)S(1)} %get-tuple-element.21), channel_id=1, source_target_pairs={{0,16},{16,0},{128,144},{144,128},{1,17},{17,1},{129,145},{145,129... | collective-permute-start | bytes 786440 | tf_op jit(solution)/shard_map/ppermute | solution.py:186
  53.6 0.7 collective-permute-start.2
  54.3 13.9 %all-to-all-done = bf16[64,2,16,128]{3,2,1,0:T(8,128)(2,1)S(1)} async-done(((bf16[64,2,16,128]{3,2,1,0:T(8,128)(2,1)}), bf16[64,2,16,128]{3,2,1,0:T(8,128)(2,1)S(1)}, u32[]{:S(2)}, u32[]{:S(2)}) %all-to-all-start) | async-done | bytes 524320 | tf_op jit(solution)/shard_map/all_to_all | solution.py:174
  68.2 0.0 collective-permute-done.3.refs_3_
  68.2 0.0 collective-permute-done.1.refs_1_
  68.2 0.0 collective-permute-done.2.refs_2_
  68.3 0.5 collective-permute-start.6
  68.7 2.2 %collective-permute-start.4 = (bf16[64,16,128]{2,1,0:T(8,128)(2,1)S(1)}, bf16[64,16,128]{2,1,0:T(8,128)(2,1)S(1)}, u32[]{:S(2)}, u32[]{:S(2)}) collective-permute-start(bf16[64,16,128]{2,1,0:T(8,128)(2,1)S(1)} %get-tuple-element.19), channel_id=1, source_target_pairs={{0,16},{16,0},{128,144},{144,128},{1,17},{17,1},{129,145},{145,129... | collective-permute-start | bytes 786440 | tf_op jit(solution)/shard_map/ppermute | solution.py:186
  70.9 0.7 collective-permute-start.5
  71.6 0.1 pad_add_fusion.where
  71.7 11.1 %collective-permute-done.6.refs_7_ = bf16[64,16,128]{2,1,0:T(8,128)(2,1)S(1)} collective-permute-done((bf16[64,16,128]{2,1,0:T(8,128)(2,1)S(1)}, bf16[64,16,128]{2,1,0:T(8,128)(2,1)S(1)}, u32[]{:S(2)}, u32[]{:S(2)}) %collective-permute-start.6) | collective-permute-done | bytes 262176 | tf_op jit(solution)/shard_map/ppermute | solution.py:186
  82.8 0.0 collective-permute-done.4.refs_5_
  82.8 0.3 collective-permute-done.5.refs_6_
  83.1 5.5 %shard_map.30 = f32[2,1,512,1024]{3,2,1,0:T(8,128)} custom-call(s32[2]{0:T(128)S(1)} %pad_add_fusion.where, bf16[64,16,128]{2,1,0:T(8,128)(2,1)S(1)} %get-tuple-element.14.refs_0_, bf16[64,16,128]{2,1,0:T(8,128)(2,1)S(1)} %collective-permute-done.1.refs_1_, bf16[64,16,128]{2,1,0:T(8,128)(2,1)S(1)} %collective-permute-done.2.refs_2_, ...), custom_call_target="tpu_custom_call" | custom-call | tf_op jit(solution)/shard_map/pallas_call | solution.py:154
  (3 shorter events, 0.1 us)
Async XLA Ops:
  0.9 13.7 %collective-permute-start = (bf16[4,8,2048]{2,1,0:T(8,128)(2,1)S(1)}, bf16[4,8,2048]{2,1,0:T(8,128)(2,1)S(1)}, u32[]{:S(2)}, u32[]{:S(2)}) collective-permute-start(bf16[4,8,2048]{2,1,0:T(8,128)(2,1)S(1)} %slice.4), channel_id=1, source_target_pairs={{0,128},{1,129},{2,130},{3,131},{4,132},{5,133},{6,134},{7,135},{8... | collective-permute-start | bytes 393224 | tf_op jit(solution)/shard_map/ppermute | solution.py:204
  14.7 12.6 %copy-start = (bf16[4,8,2048]{2,1,0:T(8,128)(2,1)}, bf16[4,8,2048]{2,1,0:T(8,128)(2,1)S(1)}, u32[]{:S(2)}) copy-start(bf16[4,8,2048]{2,1,0:T(8,128)(2,1)S(1)} %collective-permute-done.halo) | copy-start | bytes 393220
  14.7 29.9 %all-to-all-start.1 = ((bf16[64,2,16,128]{3,2,1,0:T(8,128)(2,1)}), bf16[64,2,16,128]{3,2,1,0:T(8,128)(2,1)S(1)}, u32[]{:S(2)}, u32[]{:S(2)}) async-start(bf16[64,2,16,128]{3,2,1,0:T(8,128)(2,1)} %bitcast.19), calls=%async_computation.1 | async-start | bytes 1048576 | tf_op jit(solution)/shard_map/all_to_all | solution.py:174
  44.6 23.6 %all-to-all-start = ((bf16[64,2,16,128]{3,2,1,0:T(8,128)(2,1)}), bf16[64,2,16,128]{3,2,1,0:T(8,128)(2,1)S(1)}, u32[]{:S(2)}, u32[]{:S(2)}) async-start(bf16[64,2,16,128]{3,2,1,0:T(8,128)(2,1)} %bitcast.20), calls=%async_computation | async-start | bytes 1048576 | tf_op jit(solution)/shard_map/all_to_all | solution.py:174
  51.0 17.3 %collective-permute-start.3 = (bf16[64,16,128]{2,1,0:T(8,128)(2,1)S(1)}, bf16[64,16,128]{2,1,0:T(8,128)(2,1)S(1)}, u32[]{:S(2)}, u32[]{:S(2)}) collective-permute-start(bf16[64,16,128]{2,1,0:T(8,128)(2,1)S(1)} %get-tuple-element.21), channel_id=1, source_target_pairs={{0,144},{16,128},{128,16},{144,0},{1,145},{17,129},{129,17},{145,1... | collective-permute-start | bytes 786440 | tf_op jit(solution)/shard_map/ppermute | solution.py:186
  51.4 16.8 %collective-permute-start.1 = (bf16[64,16,128]{2,1,0:T(8,128)(2,1)S(1)}, bf16[64,16,128]{2,1,0:T(8,128)(2,1)S(1)}, u32[]{:S(2)}, u32[]{:S(2)}) collective-permute-start(bf16[64,16,128]{2,1,0:T(8,128)(2,1)S(1)} %get-tuple-element.21), channel_id=1, source_target_pairs={{0,16},{16,0},{128,144},{144,128},{1,17},{17,1},{129,145},{145,129... | collective-permute-start | bytes 786440 | tf_op jit(solution)/shard_map/ppermute | solution.py:186
  53.6 14.6 %collective-permute-start.2 = (bf16[64,16,128]{2,1,0:T(8,128)(2,1)S(1)}, bf16[64,16,128]{2,1,0:T(8,128)(2,1)S(1)}, u32[]{:S(2)}, u32[]{:S(2)}) collective-permute-start(bf16[64,16,128]{2,1,0:T(8,128)(2,1)S(1)} %get-tuple-element.14.refs_0_), channel_id=1, source_target_pairs={{0,128},{16,144},{128,0},{144,16},{1,129},{17,145},{129,1},{145,17... | collective-permute-start | bytes 786440 | tf_op jit(solution)/shard_map/ppermute | solution.py:186
  68.3 14.5 %collective-permute-start.6 = (bf16[64,16,128]{2,1,0:T(8,128)(2,1)S(1)}, bf16[64,16,128]{2,1,0:T(8,128)(2,1)S(1)}, u32[]{:S(2)}, u32[]{:S(2)}) collective-permute-start(bf16[64,16,128]{2,1,0:T(8,128)(2,1)S(1)} %get-tuple-element.19), channel_id=1, source_target_pairs={{0,144},{16,128},{128,16},{144,0},{1,145},{17,129},{129,17},{145,1... | collective-permute-start | bytes 786440 | tf_op jit(solution)/shard_map/ppermute | solution.py:186
  68.7 14.1 %collective-permute-start.4 = (bf16[64,16,128]{2,1,0:T(8,128)(2,1)S(1)}, bf16[64,16,128]{2,1,0:T(8,128)(2,1)S(1)}, u32[]{:S(2)}, u32[]{:S(2)}) collective-permute-start(bf16[64,16,128]{2,1,0:T(8,128)(2,1)S(1)} %get-tuple-element.19), channel_id=1, source_target_pairs={{0,16},{16,0},{128,144},{144,128},{1,17},{17,1},{129,145},{145,129... | collective-permute-start | bytes 786440 | tf_op jit(solution)/shard_map/ppermute | solution.py:186
  70.9 12.2 %collective-permute-start.5 = (bf16[64,16,128]{2,1,0:T(8,128)(2,1)S(1)}, bf16[64,16,128]{2,1,0:T(8,128)(2,1)S(1)}, u32[]{:S(2)}, u32[]{:S(2)}) collective-permute-start(bf16[64,16,128]{2,1,0:T(8,128)(2,1)S(1)} %get-tuple-element.20.refs_4_), channel_id=1, source_target_pairs={{0,128},{16,144},{128,0},{144,16},{1,129},{17,145},{129,1},{145,17... | collective-permute-start | bytes 786440 | tf_op jit(solution)/shard_map/ppermute | solution.py:186

commit v3 on v0

v3 whole, which is shorter than its diff:
```python
import functools

import jax
import jax.numpy as jnp
import ml_dtypes
import numpy as np
from jax import lax
from jax.experimental import pallas as pl
from jax.experimental.pallas import tpu as pltpu
from jax.sharding import Mesh
from jax.sharding import PartitionSpec as P

FRAME = 2048
TAPS = 4
UNIT = 64
PIECE = 32
GROUP = 8
HALO = 4
FIRST = 3
DEPTH = 512
N_Y = 4
PLANE = ("y", "z", "core")
COLUMNS = 256
MIB = 1024 * 1024
VMEM_BANK = 56 * MIB
VMEM_VIS = 28 * MIB
F32 = jnp.float32
BF16 = jnp.bfloat16


def pfb_window():
    length = TAPS * FRAME
    points = np.arange(length, dtype=np.float64)
    window = np.sinc((points - length / 2 + 0.5) / FRAME) * (
        0.54 - 0.46 * np.cos(2.0 * np.pi * points / (length - 1))
    )
    return window.reshape(TAPS, FRAME).astype(np.float32)


def dft_table(order):
    phase = (np.arange(FRAME)[:, None] * order[None, :] % FRAME) * (2.0 * np.pi / FRAME)
    return np.concatenate([np.cos(phase), -np.sin(phase)], 1).astype(ml_dtypes.bfloat16)


def filterbank_kernel(first, halo_at, frames, halo, window, table, *refs):
    out, (held, dft, summed, turned, sem) = refs[0], refs[-5:]
    inputs = held.shape[1]
    count = out.shape[0]
    units = out.shape[1] // inputs
    span = PIECE * inputs
    pieces = UNIT // PIECE

    def copy(piece):
        return pltpu.make_async_copy(
            frames.at[pl.ds(first + piece * PIECE, PIECE)],
            held.at[pl.ds(HALO + piece * PIECE, PIECE)],
            sem.at[2 + piece],
        )

    halo_copy = pltpu.make_async_copy(
        halo.at[pl.ds(halo_at, HALO)], held.at[pl.ds(0, HALO)], sem.at[0]
    )
    table_copy = pltpu.make_async_copy(table, dft, sem.at[1])
    halo_copy.start()
    copy(0).start()
    table_copy.start()
    for piece in range(1, units * pieces):
        copy(piece).start()
    halo_copy.wait()

    table_copy.wait()

    def split(piece, lanes):
        high, rest = [], []
        for g in range(PIECE // GROUP):
            at = piece * PIECE + g * GROUP + HALO - TAPS + 1
            some = held[pl.ds(at, GROUP + TAPS - 1), :, lanes].astype(F32)
            total = window[0:1, lanes][None] * some[0:GROUP]
            for k in range(1, TAPS):
                total = total + window[k : k + 1, lanes][None] * some[k : k + GROUP]
            total = total.reshape(GROUP * inputs, DEPTH)
            high.append(total.astype(BF16))
            rest.append((total - high[-1].astype(F32)).astype(BF16))
        return jnp.concatenate(high + rest, 0)

    def body(piece, carry):
        copy(piece).wait()
        product = None
        for n in range(FRAME // DEPTH):
            lanes = slice(n * DEPTH, (n + 1) * DEPTH)
            term = jnp.dot(split(piece, lanes), dft[lanes, :], preferred_element_type=F32)
            product = term if product is None else product + term
        product = product[:span] + product[span:]
        row = pl.multiple_of(lax.rem(piece, pieces) * span, span)
        for part in range(2):
            summed[part, pl.ds(row, span), :] = product[:, part * count : (part + 1) * count]

        @pl.when(lax.rem(piece, pieces) == pieces - 1)
        def _():
            for i in range(inputs):
                both = jnp.concatenate(
                    [summed[part, pl.ds(i, UNIT, stride=inputs), :] for part in range(2)], 0
                )
                row = piece // pieces * inputs + i
                turned[pl.ds(row, count, stride=units * inputs), :] = both.T

        return carry

    lax.fori_loop(0, units * pieces, body, 0)
    out[...] = turned[...].reshape(count, units * inputs, 2 * UNIT).astype(BF16)
    for last in refs[1:-5]:
        last[...] = held[units * UNIT :]


def filterbank(frames, first, spectra, halo, halo_at, window, table, tail):
    _, inputs, _ = frames.shape
    count = table.shape[1] // 2
    units = spectra // UNIT
    there = pl.BlockSpec(memory_space=pl.ANY)
    here = pl.BlockSpec(memory_space=pltpu.VMEM)
    return pl.pallas_call(
        functools.partial(filterbank_kernel, first, halo_at),
        in_specs=[there, there, here, there],
        out_specs=[here] * (1 + tail),
        out_shape=[
            jax.ShapeDtypeStruct((count, units * inputs, 2 * UNIT), BF16),
            jax.ShapeDtypeStruct((HALO, inputs, FRAME), BF16),
        ][: 1 + tail],
        scratch_shapes=[
            pltpu.VMEM((HALO + spectra, inputs, FRAME), BF16),
            pltpu.VMEM(table.shape, BF16),
            pltpu.VMEM((2, UNIT * inputs, count), F32),
            pltpu.VMEM((count * units * inputs, 2 * UNIT), F32),
            pltpu.SemaphoreType.DMA((2 + spectra // PIECE,)),
        ],
        compiler_params=pltpu.CompilerParams(vmem_limit_bytes=VMEM_BANK),
        cost_estimate=pl.CostEstimate(
            flops=4 * spectra * inputs * FRAME * 2 * count,
            bytes_accessed=2 * spectra * inputs * FRAME + MIB,
            transcendentals=0,
        ),
    )(frames, halo, window, table)


def visibility_kernel(inputs, scale, n_sources, where, *refs):
    sources, before = refs[:n_sources], refs[n_sources:-3]
    out, right, left = refs[-3:]
    groups = sources[0].shape[0]
    n_rows = left.shape[0] // 2
    stripe = groups // N_Y * inputs
    units = right.shape[1] // (2 * 2 * UNIT)

    @pl.when(pl.program_id(0) == 0)
    def _():
        for at, source in enumerate(sources):
            per = source.shape[1] // inputs
            wide = source[...].astype(F32).reshape(groups, per, inputs, 2 * UNIT)
            for j in range(per):
                origin, u = (at * per + j) // units, (at * per + j) % units
                x_hi = (where[1] + origin % 2) % 2
                segment = (origin // 2) * units + u
                lanes = slice(segment * 2 * UNIT, (segment + 1) * 2 * UNIT)
                block = wide[:, j].reshape(groups * inputs, 2 * UNIT).astype(BF16)
                for y in range(N_Y):
                    row = pl.multiple_of((2 * y + x_hi) * stripe, stripe)
                    right[pl.ds(row, stripe), lanes] = block[y * stripe : (y + 1) * stripe]
        own = right[pl.ds(pl.multiple_of(where[0], n_rows), n_rows), :]
        left[0:n_rows, :] = own
        lane = lax.broadcasted_iota(jnp.int32, (n_rows, 2 * UNIT), 1)
        for s in range(2 * units):
            lanes = slice(s * 2 * UNIT, (s + 1) * 2 * UNIT)
            swapped = pltpu.roll(own[:, lanes].astype(F32), UNIT, 1)
            left[n_rows:, lanes] = jnp.where(lane < UNIT, swapped, -swapped).astype(BF16)

    at = pl.multiple_of(pl.program_id(0) * COLUMNS, COLUMNS)
    product = lax.dot_general(
        left[...],
        right[pl.ds(at, COLUMNS), :],
        (((1,), (1,)), ((), ())),
        preferred_element_type=F32,
    )
    for part in range(2):
        value = product[part * n_rows : (part + 1) * n_rows]
        if before:
            value = value + before[0][part, 0]
        out[part, 0] = value * scale if scale else value


def visibilities(sources, before, where, inputs, n_rows, scale):
    groups, depth, lanes = sources[0].shape
    total = 2 * groups * inputs
    length = len(sources) * depth // inputs * lanes // 2
    whole = pl.BlockSpec((groups, depth, lanes), lambda r, w: (0, 0, 0))
    block = pl.BlockSpec((2, 1, n_rows, COLUMNS), lambda r, w: (0, 0, 0, r))
    return pl.pallas_call(
        functools.partial(visibility_kernel, inputs, scale, len(sources)),
        grid_spec=pltpu.PrefetchScalarGridSpec(
            num_scalar_prefetch=1,
            grid=(total // COLUMNS,),
            in_specs=[whole] * len(sources) + [block] * len(before),
            out_specs=block,
            scratch_shapes=[
                pltpu.VMEM((total, length), BF16),
                pltpu.VMEM((2 * n_rows, length), BF16),
            ],
        ),
        out_shape=jax.ShapeDtypeStruct((2, 1, n_rows, total), F32),
        compiler_params=pltpu.CompilerParams(vmem_limit_bytes=VMEM_VIS),
        cost_estimate=pl.CostEstimate(
            flops=4 * n_rows * total * length * (1 if scale else 8),
            bytes_accessed=8 * MIB,
            transcendentals=0,
        ),
        input_output_aliases={1 + len(sources): 0} if before else {},
    )(where, *sources, *before)


def swap(array, far_x, far_t):
    route = [(t * 2 + x, (t ^ far_t) * 2 + (x ^ far_x)) for t in range(2) for x in range(2)]
    return lax.ppermute(array, ("ta", "xh"), route)


def along_x(mine, theirs):
    both = swap(theirs, 1, 1)
    far = swap(theirs, 1, 0)
    near = swap(mine, 0, 1)
    return [mine, far, near, both]


def over_plane(array):
    return lax.all_to_all(array, PLANE, split_axis=0, concat_axis=0, tiled=True)


def by_x(array, axis):
    x_hi = lax.axis_index("xh")
    return [lax.dynamic_index_in_dim(array, at, axis, keepdims=False) for at in (x_hi, 1 - x_hi)]


def local(voltages):
    inputs = voltages.shape[0]
    spectra = voltages.shape[1] // FRAME
    n_time = lax.axis_size("ta")
    n_plane = lax.axis_size(PLANE)
    n_chan = 2 * n_plane
    window = jnp.asarray(pfb_window())
    channels = np.arange(n_chan).reshape(N_Y, 2, -1).swapaxes(0, 1)
    x_first = jnp.asarray(dft_table(channels.reshape(-1)))
    x_last = jnp.asarray(dft_table(channels.reshape(2, -1).T.reshape(-1)))
    frames = voltages.reshape(inputs, spectra, FRAME).transpose(1, 0, 2)
    start = spectra // 4 * (4 - FIRST)

    late, last = filterbank(
        frames, start, spectra - start, frames, start - HALO, window, x_last, True
    )
    turned_late = over_plane(late.reshape(n_plane, 2, *late.shape[1:]))
    earlier = lax.ppermute(last, "ta", [(i, i + 1) for i in range(n_time - 1)])
    (early,) = filterbank(frames, 0, start, earlier, 0, window, x_first, False)
    sources_early = along_x(*by_x(early.reshape(2, n_plane, *early.shape[1:]), 0))
    stacked = jnp.concatenate(sources_early, 1)
    turned_late, stacked = lax.optimization_barrier((turned_late, stacked))
    sources_late = along_x(*by_x(turned_late, 1))
    turned_early = over_plane(stacked)

    n_rows = inputs * n_chan // n_time
    where = jnp.stack([lax.axis_index("ta") * n_rows, lax.axis_index("xh")]).astype(jnp.int32)
    scale = 1.0 / (16.0 * FRAME * spectra * n_time)
    so_far = visibilities(sources_late, [], where, inputs, n_rows, None)
    return visibilities([turned_early], [so_far], where, inputs, n_rows, scale)


def solution(mesh):
    fine = Mesh(mesh.devices.reshape(2, 4, 2, 8, 2), ("ta", "y", "xh", "z", "core"))
    gx = ("y", "xh", "z", "core")
    return jax.shard_map(
        local, mesh=fine, in_specs=(P(gx, "ta"),), out_specs=P(None, gx, "ta", None), check_vma=False
    )
```

time: 218 us -> 87.4 us (0.40)
  waiting for transfers between devices: 97.9 us -> 21 us
  blocking collectives: 47.4 us -> 0 us
  matrix products: 33.8 us -> 0 us
  starting transfers between devices: 4.13 us -> 37.1 us
  Pallas kernels: 0 us -> 26 us
  between operations: 13.5 us -> 0.06 us
  local copies, waits for them, and re-layouts: 12.8 us -> 1.76 us
  other arithmetic: 8.48 us -> 0.96 us
    reduce_scatter x1 -> x0, waiting for transfers between devices: 97.9 us -> none  [local(): return lax.psum_scatter(gram_sum, 'ta', scatter_dimension=2, tiled=True)]
    all_to_all x1 -> x0, blocking collectives: 47.4 us -> none  [local(): lax.all_to_all(spectra, 'gx', split_axis=1, concat_axis=2, tiled=True)]
    dot_general x5 -> x0, matrix products: 33.8 us -> none  [the longest x1 30.8 us: local(): jnp.einsum('isn,cn->cis', filtered, dft_table(n_chan), precision=lax.Prec...]
    pallas_call x0 -> x4, Pallas kernels: none -> 26 us  [the longest x2 15 us: filterbank(): pl.pallas_call(functools.partial(filterbank_kernel, first, halo_at), in_s...]
    all_to_all x0 -> x2, starting transfers between devices: none -> 26 us  [over_plane(): return lax.all_to_all(array, PLANE, split_axis=0, concat_axis=0, tiled=True)]
    reshape x2 -> x0, local copies, waits for them, and re-layouts: 11.8 us -> none  [the longest x1 11.2 us: local(): frames = voltages.reshape(in_dev, s_dev, FRAME)]
    ppermute x1 -> x7, waiting for transfers between devices: 0.01 us -> 11.5 us  [the longest x6 8.84 us: swap(): return lax.ppermute(array, ('ta', 'xh'), route)]
    all_to_all x0 -> x2, waiting for transfers between devices: none -> 9.46 us  [over_plane(): return lax.all_to_all(array, PLANE, split_axis=0, concat_axis=0, tiled=True)]
  transfers between devices with their start and end apart: 2 -> 9, of which waited for: 1 -> 6; matrix products, arithmetic and copies ran while one was open for 2% -> 2% of each run, Pallas kernels for 0% -> 12%
where the time goes in v3:
time: 87.4 us; the launch traced here: 86.9 us
  starting transfers between devices  37.1 us (42%)
  Pallas kernels  26 us (30%)
  waiting for transfers between devices  21 us (24%)
  local copies, waits for them, and re-layouts  1.76 us (2%)
  other arithmetic  0.96 us (1%)
    all_to_all x2, starting transfers between devices, over_plane(): return lax.all_to_all(array, PLANE, split_axis=0, concat_axis=0, tiled=True)  26 us
    pallas_call x2, Pallas kernels, filterbank(): pl.pallas_call(functools.partial(filterbank_kernel, first, halo_at), in_s...  15 us
    pallas_call x2, Pallas kernels, visibilities(): pl.pallas_call(functools.partial(visibility_kernel, inputs, scale, len(so...  11 us
    all_to_all x2, waiting for transfers between devices, over_plane(): return lax.all_to_all(array, PLANE, split_axis=0, concat_axis=0, tiled=True)  9.46 us
    ppermute x6, waiting for transfers between devices, swap(): return lax.ppermute(array, ('ta', 'xh'), route)  8.84 us
    ppermute x6, starting transfers between devices, swap(): return lax.ppermute(array, ('ta', 'xh'), route)  7.98 us
    ppermute x1, starting transfers between devices, local(): earlier = lax.ppermute(last, 'ta', [(i, i + 1) for i in range(n_time - 1)])  3.12 us
    ppermute x1, waiting for transfers between devices, local(): earlier = lax.ppermute(last, 'ta', [(i, i + 1) for i in range(n_time - 1)])  2.7 us
  transfers between devices with their start and end apart: 9, of which 6 were waited for; matrix products, arithmetic and copies ran while one was open for 2% of the time, Pallas kernels for 12%

profile of v3, /device:TPU:1, one launch (start us, length us, event | category | flops | bytes accessed | tf_op | source)
XLA Modules:
  0.0 86.9 jit_solution(5955777504611392862)
XLA Ops:
  0.0 9.8 %shard_map.46 = (bf16[128,24,128]{2,1,0:T(8,128)(2,1)}, bf16[4,8,2048]{2,1,0:T(8,128)(2,1)}) custom-call(bf16[256,8,2048]{2,1,0:T(8,128)(2,1)} %bitcast.15, bf16[256,8,2048]{2,1,0:T(8,128)(2,1)} %bitcast.16, f32[4,2048]{1,0:T(4,128)} %constant.36.clone.window, bf16[2048,256]{1,0:T(8,128)(2,1)} %constant.38.clone.table), custom_call_target="tpu_custom_call" | custom-call | flops 3221225472 | bytes 7340032 | tf_op jit(solution)/shard_map/pallas_call | solution.py:121
  9.8 13.2 %all-to-all-start = ((bf16[64,2,24,128]{3,2,1,0:T(8,128)(2,1)}), bf16[64,2,24,128]{3,2,1,0:T(8,128)(2,1)S(1)}, u32[]{:S(2)}, u32[]{:S(2)}) async-start(bf16[64,2,24,128]{3,2,1,0:T(8,128)(2,1)} %bitcast.19), calls=%async_computation | async-start | bytes 1572864 | tf_op jit(solution)/shard_map/all_to_all | solution.py:231
  23.0 3.1 %collective-permute-start = (bf16[4,8,2048]{2,1,0:T(8,128)(2,1)}, bf16[4,8,2048]{2,1,0:T(8,128)(2,1)S(1)}, u32[]{:S(2)}, u32[]{:S(2)}) collective-permute-start(bf16[4,8,2048]{2,1,0:T(8,128)(2,1)} %get-tuple-element.10), channel_id=1, source_target_pairs={{0,128},{1,129},{2,130},{3,131},{4,132},{5,133},{6,134},{7,135},{8... | collective-permute-start | bytes 393224 | tf_op jit(solution)/shard_map/ppermute | solution.py:256
  26.1 2.7 %collective-permute-done.halo = bf16[4,8,2048]{2,1,0:T(8,128)(2,1)S(1)} collective-permute-done((bf16[4,8,2048]{2,1,0:T(8,128)(2,1)}, bf16[4,8,2048]{2,1,0:T(8,128)(2,1)S(1)}, u32[]{:S(2)}, u32[]{:S(2)}) %collective-permute-start) | collective-permute-done | bytes 131104 | tf_op jit(solution)/shard_map/ppermute | solution.py:256
  28.8 0.6 copy-done
  29.5 5.3 %shard_map.47 = bf16[128,8,128]{2,1,0:T(8,128)(2,1)} custom-call(bf16[256,8,2048]{2,1,0:T(8,128)(2,1)} %bitcast.17, bf16[4,8,2048]{2,1,0:T(8,128)(2,1)} %copy-done, f32[4,2048]{1,0:T(4,128)} %constant.36.clone.window, bf16[2048,256]{1,0:T(8,128)(2,1)} %constant.37.clone.table), custom_call_target="tpu_custom_call" | custom-call | flops 1073741824 | bytes 3145728 | tf_op jit(solution)/shard_map/pallas_call | solution.py:121
  34.7 1.0 %dynamic-slice_bitcast_fusion.3 = (bf16[64,8,128]{2,1,0:T(8,128)(2,1)S(1)}, bf16[64,8,128]{2,1,0:T(8,128)(2,1)S(1)}) fusion(bf16[2,64,8,128]{3,2,1,0:T(8,128)(2,1)} %bitcast.18, s32[]{:T(128)S(6)} %select_n.10, s32[]{:T(128)S(6)} %select_n.11), kind=kLoop, calls=%fused_computation.4 | loop fusion | bytes 524296 | tf_op jit(solution)/shard_map/jit(dynamic_index_in_dim)/squeeze | solution.py:236
  35.7 2.2 %collective-permute-start.2 = (bf16[64,8,128]{2,1,0:T(8,128)(2,1)S(1)}, bf16[64,8,128]{2,1,0:T(8,128)(2,1)S(1)}, u32[]{:S(2)}, u32[]{:S(2)}) collective-permute-start(bf16[64,8,128]{2,1,0:T(8,128)(2,1)S(1)} %get-tuple-element.15), channel_id=1, source_target_pairs={{0,128},{16,144},{128,0},{144,16},{1,129},{17,145},{129,1},{145,17... | collective-permute-start | bytes 393224 | tf_op jit(solution)/shard_map/ppermute | solution.py:220
  37.9 1.4 %collective-permute-start.3 = (bf16[64,8,128]{2,1,0:T(8,128)(2,1)S(1)}, bf16[64,8,128]{2,1,0:T(8,128)(2,1)S(1)}, u32[]{:S(2)}, u32[]{:S(2)}) collective-permute-start(bf16[64,8,128]{2,1,0:T(8,128)(2,1)S(1)} %get-tuple-element.16), channel_id=1, source_target_pairs={{0,144},{16,128},{128,16},{144,0},{1,145},{17,129},{129,17},{145,1... | collective-permute-start | bytes 393224 | tf_op jit(solution)/shard_map/ppermute | solution.py:220
  39.3 1.1 %collective-permute-start.1 = (bf16[64,8,128]{2,1,0:T(8,128)(2,1)S(1)}, bf16[64,8,128]{2,1,0:T(8,128)(2,1)S(1)}, u32[]{:S(2)}, u32[]{:S(2)}) collective-permute-start(bf16[64,8,128]{2,1,0:T(8,128)(2,1)S(1)} %get-tuple-element.16), channel_id=1, source_target_pairs={{0,16},{16,0},{128,144},{144,128},{1,17},{17,1},{129,145},{145,129... | collective-permute-start | bytes 393224 | tf_op jit(solution)/shard_map/ppermute | solution.py:220
  40.4 0.2 collective-permute-done.2
  40.6 2.7 %collective-permute-done.3 = bf16[64,8,128]{2,1,0:T(8,128)(2,1)S(1)} collective-permute-done((bf16[64,8,128]{2,1,0:T(8,128)(2,1)S(1)}, bf16[64,8,128]{2,1,0:T(8,128)(2,1)S(1)}, u32[]{:S(2)}, u32[]{:S(2)}) %collective-permute-start.3) | collective-permute-done | bytes 131104 | tf_op jit(solution)/shard_map/ppermute | solution.py:220
  43.2 3.1 %collective-permute-done.1 = bf16[64,8,128]{2,1,0:T(8,128)(2,1)S(1)} collective-permute-done((bf16[64,8,128]{2,1,0:T(8,128)(2,1)S(1)}, bf16[64,8,128]{2,1,0:T(8,128)(2,1)S(1)}, u32[]{:S(2)}, u32[]{:S(2)}) %collective-permute-start.1) | collective-permute-done | bytes 131104 | tf_op jit(solution)/shard_map/ppermute | solution.py:220
  46.3 0.9 %pad_maximum_fusion = bf16[64,32,128]{2,1,0:T(8,128)(2,1)} fusion(bf16[64,8,128]{2,1,0:T(8,128)(2,1)S(1)} %collective-permute-done.3, bf16[64,8,128]{2,1,0:T(8,128)(2,1)S(1)} %collective-permute-done.2, bf16[64,8,128]{2,1,0:T(8,128)(2,1)S(1)} %collective-permute-done.1, bf16[64,8,128]{2,1,0:T(8,128)(2,1)S(1)} %get-tuple-element.15), kind=kLoop, calls=%fused_computation | loop fusion | flops 2097152 | bytes 1048576 | tf_op jit(solution)/shard_map/concatenate | solution.py:259
  47.2 0.1 dynamic-slice_bitcast_fusion
  47.3 1.3 %collective-permute-start.6 = (bf16[64,24,128]{2,1,0:T(8,128)(2,1)S(1)}, bf16[64,24,128]{2,1,0:T(8,128)(2,1)S(1)}, u32[]{:S(2)}, u32[]{:S(2)}) collective-permute-start(bf16[64,24,128]{2,1,0:T(8,128)(2,1)S(1)} %get-tuple-element.13), channel_id=1, source_target_pairs={{0,144},{16,128},{128,16},{144,0},{1,145},{17,129},{129,17},{145,1... | collective-permute-start | bytes 1179656 | tf_op jit(solution)/shard_map/ppermute | solution.py:220
  48.6 0.6 collective-permute-start.4
  49.2 1.5 %collective-permute-start.5 = (bf16[64,24,128]{2,1,0:T(8,128)(2,1)S(1)}, bf16[64,24,128]{2,1,0:T(8,128)(2,1)S(1)}, u32[]{:S(2)}, u32[]{:S(2)}) collective-permute-start(bf16[64,24,128]{2,1,0:T(8,128)(2,1)S(1)} %get-tuple-element.14.refs_0_), channel_id=1, source_target_pairs={{0,128},{16,144},{128,0},{144,16},{1,129},{17,145},{129,1},{145,17... | collective-permute-start | bytes 1179656 | tf_op jit(solution)/shard_map/ppermute | solution.py:220
  50.6 0.1 pad_add_fusion.where
  50.7 12.8 %all-to-all-start.1 = ((bf16[64,32,128]{2,1,0:T(8,128)(2,1)}), bf16[64,32,128]{2,1,0:T(8,128)(2,1)S(1)}, u32[]{:S(2)}, u32[]{:S(2)}) async-start(bf16[64,32,128]{2,1,0:T(8,128)(2,1)} %pad_maximum_fusion), calls=%async_computation.1 | async-start | bytes 1048576 | tf_op jit(solution)/shard_map/all_to_all | solution.py:231
  63.6 2.9 %collective-permute-done.6.refs_3_ = bf16[64,24,128]{2,1,0:T(8,128)(2,1)S(1)} collective-permute-done((bf16[64,24,128]{2,1,0:T(8,128)(2,1)S(1)}, bf16[64,24,128]{2,1,0:T(8,128)(2,1)S(1)}, u32[]{:S(2)}, u32[]{:S(2)}) %collective-permute-start.6) | collective-permute-done | bytes 393248 | tf_op jit(solution)/shard_map/ppermute | solution.py:220
  66.5 5.0 %shard_map.48.refs_1_ = f32[2,1,512,1024]{3,2,1,0:T(8,128)} custom-call(s32[2]{0:T(128)S(1)} %pad_add_fusion.where, bf16[64,24,128]{2,1,0:T(8,128)(2,1)S(1)} %get-tuple-element.14.refs_0_, bf16[64,24,128]{2,1,0:T(8,128)(2,1)S(1)} %collective-permute-done.4.refs_1_, bf16[64,24,128]{2,1,0:T(8,128)(2,1)S(1)} %collective-permute-done.5.refs_2_, ...), custom_call_target="tpu_custom_call" | custom-call | flops 12884901888 | bytes 8388608 | tf_op jit(solution)/shard_map/pallas_call | solution.py:195
  71.4 9.5 %all-to-all-done.1.refs_0_ = bf16[64,32,128]{2,1,0:T(8,128)(2,1)S(1)} async-done(((bf16[64,32,128]{2,1,0:T(8,128)(2,1)}), bf16[64,32,128]{2,1,0:T(8,128)(2,1)S(1)}, u32[]{:S(2)}, u32[]{:S(2)}) %all-to-all-start.1) | async-done | bytes 524320 | tf_op jit(solution)/shard_map/all_to_all | solution.py:231
  80.9 6.0 %shard_map.49 = f32[2,1,512,1024]{3,2,1,0:T(8,128)} custom-call(s32[2]{0:T(128)S(1)} %pad_add_fusion.where, bf16[64,32,128]{2,1,0:T(8,128)(2,1)S(1)} %all-to-all-done.1.refs_0_, f32[2,1,512,1024]{3,2,1,0:T(8,128)} %shard_map.48.refs_1_), custom_call_target="tpu_custom_call", output_to_operand_aliasing={{}: (2, {})} | custom-call | flops 536870912 | bytes 8388608 | tf_op jit(solution)/shard_map/pallas_call | solution.py:195
  (4 shorter events, 0.0 us)
Async XLA Ops:
  9.8 37.4 %all-to-all-start = ((bf16[64,2,24,128]{3,2,1,0:T(8,128)(2,1)}), bf16[64,2,24,128]{3,2,1,0:T(8,128)(2,1)S(1)}, u32[]{:S(2)}, u32[]{:S(2)}) async-start(bf16[64,2,24,128]{3,2,1,0:T(8,128)(2,1)} %bitcast.19), calls=%async_computation | async-start | bytes 1572864 | tf_op jit(solution)/shard_map/all_to_all | solution.py:231
  23.0 5.8 %collective-permute-start = (bf16[4,8,2048]{2,1,0:T(8,128)(2,1)}, bf16[4,8,2048]{2,1,0:T(8,128)(2,1)S(1)}, u32[]{:S(2)}, u32[]{:S(2)}) collective-permute-start(bf16[4,8,2048]{2,1,0:T(8,128)(2,1)} %get-tuple-element.10), channel_id=1, source_target_pairs={{0,128},{1,129},{2,130},{3,131},{4,132},{5,133},{6,134},{7,135},{8... | collective-permute-start | bytes 393224 | tf_op jit(solution)/shard_map/ppermute | solution.py:256
  28.8 0.7 copy-start
  35.7 4.8 %collective-permute-start.2 = (bf16[64,8,128]{2,1,0:T(8,128)(2,1)S(1)}, bf16[64,8,128]{2,1,0:T(8,128)(2,1)S(1)}, u32[]{:S(2)}, u32[]{:S(2)}) collective-permute-start(bf16[64,8,128]{2,1,0:T(8,128)(2,1)S(1)} %get-tuple-element.15), channel_id=1, source_target_pairs={{0,128},{16,144},{128,0},{144,16},{1,129},{17,145},{129,1},{145,17... | collective-permute-start | bytes 393224 | tf_op jit(solution)/shard_map/ppermute | solution.py:220
  37.9 5.3 %collective-permute-start.3 = (bf16[64,8,128]{2,1,0:T(8,128)(2,1)S(1)}, bf16[64,8,128]{2,1,0:T(8,128)(2,1)S(1)}, u32[]{:S(2)}, u32[]{:S(2)}) collective-permute-start(bf16[64,8,128]{2,1,0:T(8,128)(2,1)S(1)} %get-tuple-element.16), channel_id=1, source_target_pairs={{0,144},{16,128},{128,16},{144,0},{1,145},{17,129},{129,17},{145,1... | collective-permute-start | bytes 393224 | tf_op jit(solution)/shard_map/ppermute | solution.py:220
  39.3 7.0 %collective-permute-start.1 = (bf16[64,8,128]{2,1,0:T(8,128)(2,1)S(1)}, bf16[64,8,128]{2,1,0:T(8,128)(2,1)S(1)}, u32[]{:S(2)}, u32[]{:S(2)}) collective-permute-start(bf16[64,8,128]{2,1,0:T(8,128)(2,1)S(1)} %get-tuple-element.16), channel_id=1, source_target_pairs={{0,16},{16,0},{128,144},{144,128},{1,17},{17,1},{129,145},{145,129... | collective-permute-start | bytes 393224 | tf_op jit(solution)/shard_map/ppermute | solution.py:220
  47.3 19.2 %collective-permute-start.6 = (bf16[64,24,128]{2,1,0:T(8,128)(2,1)S(1)}, bf16[64,24,128]{2,1,0:T(8,128)(2,1)S(1)}, u32[]{:S(2)}, u32[]{:S(2)}) collective-permute-start(bf16[64,24,128]{2,1,0:T(8,128)(2,1)S(1)} %get-tuple-element.13), channel_id=1, source_target_pairs={{0,144},{16,128},{128,16},{144,0},{1,145},{17,129},{129,17},{145,1... | collective-permute-start | bytes 1179656 | tf_op jit(solution)/shard_map/ppermute | solution.py:220
  48.6 17.9 %collective-permute-start.4 = (bf16[64,24,128]{2,1,0:T(8,128)(2,1)S(1)}, bf16[64,24,128]{2,1,0:T(8,128)(2,1)S(1)}, u32[]{:S(2)}, u32[]{:S(2)}) collective-permute-start(bf16[64,24,128]{2,1,0:T(8,128)(2,1)S(1)} %get-tuple-element.13), channel_id=1, source_target_pairs={{0,16},{16,0},{128,144},{144,128},{1,17},{17,1},{129,145},{145,129... | collective-permute-start | bytes 1179656 | tf_op jit(solution)/shard_map/ppermute | solution.py:220
  49.2 17.3 %collective-permute-start.5 = (bf16[64,24,128]{2,1,0:T(8,128)(2,1)S(1)}, bf16[64,24,128]{2,1,0:T(8,128)(2,1)S(1)}, u32[]{:S(2)}, u32[]{:S(2)}) collective-permute-start(bf16[64,24,128]{2,1,0:T(8,128)(2,1)S(1)} %get-tuple-element.14.refs_0_), channel_id=1, source_target_pairs={{0,128},{16,144},{128,0},{144,16},{1,129},{17,145},{129,1},{145,17... | collective-permute-start | bytes 1179656 | tf_op jit(solution)/shard_map/ppermute | solution.py:220
  50.7 30.2 %all-to-all-start.1 = ((bf16[64,32,128]{2,1,0:T(8,128)(2,1)}), bf16[64,32,128]{2,1,0:T(8,128)(2,1)S(1)}, u32[]{:S(2)}, u32[]{:S(2)}) async-start(bf16[64,32,128]{2,1,0:T(8,128)(2,1)} %pad_maximum_fusion), calls=%async_computation.1 | async-start | bytes 1048576 | tf_op jit(solution)/shard_map/all_to_all | solution.py:231

commit v4 on v3

--- a/solution.py
+++ b/solution.py
@@ -20,6 +20,8 @@
 DEPTH = 512
 N_Y = 4
 PLANE = ("y", "z", "core")
+BANK_FLOPS = 20 * 1024**3
+ROWS_FLOPS = 9 * 1024**3
 COLUMNS = 256
 MIB = 1024 * 1024
 VMEM_BANK = 56 * MIB
@@ -135,40 +137,67 @@
         ],
         compiler_params=pltpu.CompilerParams(vmem_limit_bytes=VMEM_BANK),
         cost_estimate=pl.CostEstimate(
-            flops=4 * spectra * inputs * FRAME * 2 * count,
+            flops=BANK_FLOPS,
             bytes_accessed=2 * spectra * inputs * FRAME + MIB,
             transcendentals=0,
         ),
     )(frames, halo, window, table)
 
 
-def visibility_kernel(inputs, scale, n_sources, where, *refs):
-    sources, before = refs[:n_sources], refs[n_sources:-3]
-    out, right, left = refs[-3:]
-    groups = sources[0].shape[0]
+def rows_kernel(inputs, source, out):
+    groups, depth, _ = source.shape
+    units = depth // inputs
+    wide = source[...].astype(F32).reshape(groups, units, inputs, 2 * UNIT)
+    for u in range(units):
+        rows = wide[:, u].reshape(groups * inputs, 2 * UNIT).astype(BF16)
+        out[u * groups * inputs : (u + 1) * groups * inputs, :] = rows
+
+
+def as_rows(source, inputs):
+    groups, depth, lanes = source.shape
+    here = pl.BlockSpec(memory_space=pltpu.VMEM)
+    return pl.pallas_call(
+        functools.partial(rows_kernel, inputs),
+        in_specs=[here],
+        out_specs=here,
+        out_shape=jax.ShapeDtypeStruct((groups * depth, lanes), BF16),
+        compiler_params=pltpu.CompilerParams(vmem_limit_bytes=VMEM_VIS),
+        cost_estimate=pl.CostEstimate(flops=ROWS_FLOPS, bytes_accessed=MIB, transcendentals=0),
+    )(source)
+
+
+def visibility_kernel(inputs, scale, where, mine, far, near, both, small, out, right, left):
+    groups = mine.shape[0]
+    units = mine.shape[1] // inputs
     n_rows = left.shape[0] // 2
     stripe = groups // N_Y * inputs
-    units = right.shape[1] // (2 * 2 * UNIT)
+    n_lanes = 2 * UNIT
+
+    def place(rows, origin, unit):
+        x_hi = (where[1] + origin % 2) % 2
+        segment = origin // 2 * (units + 1) + unit
+        for y in range(N_Y):
+            row = pl.multiple_of((2 * y + x_hi) * stripe, stripe)
+            right[pl.ds(row, stripe), segment * n_lanes : (segment + 1) * n_lanes] = rows[
+                y * stripe : (y + 1) * stripe
+            ]
 
     @pl.when(pl.program_id(0) == 0)
     def _():
-        for at, source in enumerate(sources):
-            per = source.shape[1] // inputs
-            wide = source[...].astype(F32).reshape(groups, per, inputs, 2 * UNIT)
-            for j in range(per):
-                origin, u = (at * per + j) // units, (at * per + j) % units
-                x_hi = (where[1] + origin % 2) % 2
-                segment = (origin // 2) * units + u
-                lanes = slice(segment * 2 * UNIT, (segment + 1) * 2 * UNIT)
-                block = wide[:, j].reshape(groups * inputs, 2 * UNIT).astype(BF16)
-                for y in range(N_Y):
-                    row = pl.multiple_of((2 * y + x_hi) * stripe, stripe)
-                    right[pl.ds(row, stripe), lanes] = block[y * stripe : (y + 1) * stripe]
-        own = right[pl.ds(pl.multiple_of(where[0], n_rows), n_rows), :]
+        for origin, source in ((0, mine), (2, near), (3, both)):
+            wide = source[...].astype(F32).reshape(groups, units, inputs, n_lanes)
+            for u in range(units):
+                place(wide[:, u].reshape(groups * inputs, n_lanes).astype(BF16), origin, u)
+        for u in range(units):
+            place(far[u * groups * inputs : (u + 1) * groups * inputs, :], 1, u)
+        wide = small[...].astype(F32).reshape(groups, 4, inputs, n_lanes)
+        for origin in range(4):
+            place(wide[:, origin].reshape(groups * inputs, n_lanes).astype(BF16), origin, units)
+        own = right[pl.ds(pl.multiple_of(where[0] * n_rows, n_rows), n_rows), :]
         left[0:n_rows, :] = own
-        lane = lax.broadcasted_iota(jnp.int32, (n_rows, 2 * UNIT), 1)
-        for s in range(2 * units):
-            lanes = slice(s * 2 * UNIT, (s + 1) * 2 * UNIT)
+        lane = lax.broadcasted_iota(jnp.int32, (n_rows, n_lanes), 1)
+        for s in range(right.shape[1] // n_lanes):
+            lanes = slice(s * n_lanes, (s + 1) * n_lanes)
             swapped = pltpu.roll(own[:, lanes].astype(F32), UNIT, 1)
             left[n_rows:, lanes] = jnp.where(lane < UNIT, swapped, -swapped).astype(BF16)
 
@@ -180,39 +209,30 @@
         preferred_element_type=F32,
     )
     for part in range(2):
-        value = product[part * n_rows : (part + 1) * n_rows]
-        if before:
-            value = value + before[0][part, 0]
-        out[part, 0] = value * scale if scale else value
-
-
-def visibilities(sources, before, where, inputs, n_rows, scale):
+        out[part, 0] = product[part * n_rows : (part + 1) * n_rows] * scale
+
+
+def visibilities(where, sources, inputs, scale):
     groups, depth, lanes = sources[0].shape
     total = 2 * groups * inputs
-    length = len(sources) * depth // inputs * lanes // 2
-    whole = pl.BlockSpec((groups, depth, lanes), lambda r, w: (0, 0, 0))
-    block = pl.BlockSpec((2, 1, n_rows, COLUMNS), lambda r, w: (0, 0, 0, r))
+    length = 2 * (depth // inputs + 1) * lanes
     return pl.pallas_call(
-        functools.partial(visibility_kernel, inputs, scale, len(sources)),
+        functools.partial(visibility_kernel, inputs, scale),
         grid_spec=pltpu.PrefetchScalarGridSpec(
             num_scalar_prefetch=1,
             grid=(total // COLUMNS,),
-            in_specs=[whole] * len(sources) + [block] * len(before),
-            out_specs=block,
-            scratch_shapes=[
-                pltpu.VMEM((total, length), BF16),
-                pltpu.VMEM((2 * n_rows, length), BF16),
+            in_specs=[
+                pl.BlockSpec(source.shape, lambda r, w, n=source.ndim: (0,) * n) for source in sources
             ],
+            out_specs=pl.BlockSpec((2, 1, total // 2, COLUMNS), lambda r, w: (0, 0, 0, r)),
+            scratch_shapes=[pltpu.VMEM((total, length), BF16), pltpu.VMEM((total, length), BF16)],
         ),
-        out_shape=jax.ShapeDtypeStruct((2, 1, n_rows, total), F32),
+        out_shape=jax.ShapeDtypeStruct((2, 1, total // 2, total), F32),
         compiler_params=pltpu.CompilerParams(vmem_limit_bytes=VMEM_VIS),
         cost_estimate=pl.CostEstimate(
-            flops=4 * n_rows * total * length * (1 if scale else 8),
-            bytes_accessed=8 * MIB,
-            transcendentals=0,
+            flops=2 * total * total * length, bytes_accessed=7 * MIB, transcendentals=0
         ),
-        input_output_aliases={1 + len(sources): 0} if before else {},
-    )(where, *sources, *before)
+    )(where, *sources)
 
 
 def swap(array, far_x, far_t):
@@ -261,11 +281,11 @@
     sources_late = along_x(*by_x(turned_late, 1))
     turned_early = over_plane(stacked)
 
-    n_rows = inputs * n_chan // n_time
-    where = jnp.stack([lax.axis_index("ta") * n_rows, lax.axis_index("xh")]).astype(jnp.int32)
+    where = jnp.stack([lax.axis_index("ta"), lax.axis_index("xh")]).astype(jnp.int32)
     scale = 1.0 / (16.0 * FRAME * spectra * n_time)
-    so_far = visibilities(sources_late, [], where, inputs, n_rows, None)
-    return visibilities([turned_early], [so_far], where, inputs, n_rows, scale)
+    mine, far, near, both = sources_late
+    far = as_rows(far, inputs)
+    return visibilities(where, [mine, far, near, both, turned_early], inputs, scale)
 
 
 def solution(mesh):

time: 87.4 us -> 82.1 us (0.939)
  starting transfers between devices: 37.1 us -> 29.1 us
  waiting for transfers between devices: 21 us -> 28.7 us
  Pallas kernels: 26 us -> 21 us
    ppermute x6, waiting for transfers between devices: 8.84 us -> 16.2 us  [swap(): return lax.ppermute(array, ('ta', 'xh'), route)]
    all_to_all x2, starting transfers between devices: 26 us -> 19.1 us  [over_plane(): return lax.all_to_all(array, PLANE, split_axis=0, concat_axis=0, tiled=True)]
    pallas_call x2, Pallas kernels: 11 us -> 5.92 us  [the longest x1 5.85 us: visibilities(): pl.pallas_call(functools.partial(visibility_kernel, inputs, scale), grid_...]
    all_to_all x2, waiting for transfers between devices: 9.46 us -> 12.5 us  [over_plane(): return lax.all_to_all(array, PLANE, split_axis=0, concat_axis=0, tiled=True)]
    ppermute x1, waiting for transfers between devices: 2.7 us -> 0.01 us  [local(): earlier = lax.ppermute(last, 'ta', [(i, i + 1) for i in range(n_time - 1)])]
    ppermute x6, starting transfers between devices: 7.98 us -> 6.09 us  [swap(): return lax.ppermute(array, ('ta', 'xh'), route)]
  transfers between devices with their start and end apart: 9 -> 9, of which waited for: 6 -> 7; matrix products, arithmetic and copies ran while one was open for 2% -> 2% of each run, Pallas kernels for 12% -> 7%
where the time goes in v4:
time: 82.1 us; the launch traced here: 81.6 us
  starting transfers between devices  29.1 us (35%)
  waiting for transfers between devices  28.7 us (35%)
  Pallas kernels  21 us (26%)
  local copies, waits for them, and re-layouts  1.75 us (2%)
  other arithmetic  0.96 us (1%)
    all_to_all x2, starting transfers between devices, over_plane(): return lax.all_to_all(array, PLANE, split_axis=0, concat_axis=0, tiled=True)  19.1 us
    ppermute x6, waiting for transfers between devices, swap(): return lax.ppermute(array, ('ta', 'xh'), route)  16.2 us
    pallas_call x2, Pallas kernels, filterbank(): pl.pallas_call(functools.partial(filterbank_kernel, first, halo_at), in_s...  15 us
    all_to_all x2, waiting for transfers between devices, over_plane(): return lax.all_to_all(array, PLANE, split_axis=0, concat_axis=0, tiled=True)  12.5 us
    ppermute x6, starting transfers between devices, swap(): return lax.ppermute(array, ('ta', 'xh'), route)  6.09 us
    pallas_call x1, Pallas kernels, visibilities(): pl.pallas_call(functools.partial(visibility_kernel, inputs, scale), grid_...  5.85 us
    ppermute x1, starting transfers between devices, local(): earlier = lax.ppermute(last, 'ta', [(i, i + 1) for i in range(n_time - 1)])  3.95 us
  transfers between devices with their start and end apart: 9, of which 7 were waited for; matrix products, arithmetic and copies ran while one was open for 2% of the time, Pallas kernels for 7%

profile of v4, /device:TPU:1, one launch (start us, length us, event | category | flops | bytes accessed | tf_op | source)
XLA Modules:
  0.0 81.6 jit_solution(4569411178334615367)
XLA Ops:
  0.0 9.8 %shard_map.46 = (bf16[128,24,128]{2,1,0:T(8,128)(2,1)}, bf16[4,8,2048]{2,1,0:T(8,128)(2,1)}) custom-call(bf16[256,8,2048]{2,1,0:T(8,128)(2,1)} %bitcast.17, bf16[256,8,2048]{2,1,0:T(8,128)(2,1)} %bitcast.18, f32[4,2048]{1,0:T(4,128)} %constant.34.clone.window, bf16[2048,256]{1,0:T(8,128)(2,1)} %constant.36.clone.table), custom_call_target="tpu_custom_call" | custom-call | flops 21474836480 | bytes 7340032 | tf_op jit(solution)/shard_map/pallas_call | solution.py:123
  9.8 4.0 %collective-permute-start = (bf16[4,8,2048]{2,1,0:T(8,128)(2,1)}, bf16[4,8,2048]{2,1,0:T(8,128)(2,1)S(1)}, u32[]{:S(2)}, u32[]{:S(2)}) collective-permute-start(bf16[4,8,2048]{2,1,0:T(8,128)(2,1)} %get-tuple-element.10), channel_id=1, source_target_pairs={{0,128},{1,129},{2,130},{3,131},{4,132},{5,133},{6,134},{7,135},{8... | collective-permute-start | bytes 393224 | tf_op jit(solution)/shard_map/ppermute | solution.py:276
  13.8 12.6 %all-to-all-start = ((bf16[64,2,24,128]{3,2,1,0:T(8,128)(2,1)}), bf16[64,2,24,128]{3,2,1,0:T(8,128)(2,1)S(1)}, u32[]{:S(2)}, u32[]{:S(2)}) async-start(bf16[64,2,24,128]{3,2,1,0:T(8,128)(2,1)} %bitcast.15), calls=%async_computation | async-start | bytes 1572864 | tf_op jit(solution)/shard_map/all_to_all | solution.py:251
  26.4 0.6 copy-done
  27.1 5.3 %shard_map.47 = bf16[128,8,128]{2,1,0:T(8,128)(2,1)} custom-call(bf16[256,8,2048]{2,1,0:T(8,128)(2,1)} %bitcast.19, bf16[4,8,2048]{2,1,0:T(8,128)(2,1)} %copy-done, f32[4,2048]{1,0:T(4,128)} %constant.34.clone.window, bf16[2048,256]{1,0:T(8,128)(2,1)} %constant.35.clone.table), custom_call_target="tpu_custom_call" | custom-call | flops 21474836480 | bytes 3145728 | tf_op jit(solution)/shard_map/pallas_call | solution.py:123
  32.3 1.0 %dynamic-slice_bitcast_fusion.3 = (bf16[64,8,128]{2,1,0:T(8,128)(2,1)S(1)}, bf16[64,8,128]{2,1,0:T(8,128)(2,1)S(1)}) fusion(bf16[2,64,8,128]{3,2,1,0:T(8,128)(2,1)} %bitcast.16, s32[]{:T(128)S(6)} %select_n.10, s32[]{:T(128)S(6)} %select_n.11), kind=kLoop, calls=%fused_computation.4 | loop fusion | bytes 524296 | tf_op jit(solution)/shard_map/jit(dynamic_index_in_dim)/squeeze | solution.py:256
  33.3 0.1 collective-permute-start.2
  33.4 2.7 %collective-permute-start.3 = (bf16[64,8,128]{2,1,0:T(8,128)(2,1)S(1)}, bf16[64,8,128]{2,1,0:T(8,128)(2,1)S(1)}, u32[]{:S(2)}, u32[]{:S(2)}) collective-permute-start(bf16[64,8,128]{2,1,0:T(8,128)(2,1)S(1)} %get-tuple-element.16), channel_id=1, source_target_pairs={{0,144},{16,128},{128,16},{144,0},{1,145},{17,129},{129,17},{145,1... | collective-permute-start | bytes 393224 | tf_op jit(solution)/shard_map/ppermute | solution.py:240
  36.1 0.5 collective-permute-start.1
  36.7 1.4 %collective-permute-done.2 = bf16[64,8,128]{2,1,0:T(8,128)(2,1)S(1)} collective-permute-done((bf16[64,8,128]{2,1,0:T(8,128)(2,1)S(1)}, bf16[64,8,128]{2,1,0:T(8,128)(2,1)S(1)}, u32[]{:S(2)}, u32[]{:S(2)}) %collective-permute-start.2) | collective-permute-done | bytes 131104 | tf_op jit(solution)/shard_map/ppermute | solution.py:240
  38.0 3.3 %collective-permute-done.3 = bf16[64,8,128]{2,1,0:T(8,128)(2,1)S(1)} collective-permute-done((bf16[64,8,128]{2,1,0:T(8,128)(2,1)S(1)}, bf16[64,8,128]{2,1,0:T(8,128)(2,1)S(1)}, u32[]{:S(2)}, u32[]{:S(2)}) %collective-permute-start.3) | collective-permute-done | bytes 131104 | tf_op jit(solution)/shard_map/ppermute | solution.py:240
  41.3 0.4 collective-permute-done.1
  41.8 0.9 %pad_maximum_fusion = bf16[64,32,128]{2,1,0:T(8,128)(2,1)} fusion(bf16[64,8,128]{2,1,0:T(8,128)(2,1)S(1)} %collective-permute-done.3, bf16[64,8,128]{2,1,0:T(8,128)(2,1)S(1)} %collective-permute-done.2, bf16[64,8,128]{2,1,0:T(8,128)(2,1)S(1)} %collective-permute-done.1, bf16[64,8,128]{2,1,0:T(8,128)(2,1)S(1)} %get-tuple-element.15), kind=kLoop, calls=%fused_computation | loop fusion | flops 2097152 | bytes 1048576 | tf_op jit(solution)/shard_map/concatenate | solution.py:279
  42.6 6.7 %all-to-all-done = bf16[64,2,24,128]{3,2,1,0:T(8,128)(2,1)S(1)} async-done(((bf16[64,2,24,128]{3,2,1,0:T(8,128)(2,1)}), bf16[64,2,24,128]{3,2,1,0:T(8,128)(2,1)S(1)}, u32[]{:S(2)}, u32[]{:S(2)}) %all-to-all-start) | async-done | bytes 786464 | tf_op jit(solution)/shard_map/all_to_all | solution.py:251
  49.4 0.1 dynamic-slice_bitcast_fusion
  49.5 2.5 %collective-permute-start.4 = (bf16[64,24,128]{2,1,0:T(8,128)(2,1)S(1)}, bf16[64,24,128]{2,1,0:T(8,128)(2,1)S(1)}, u32[]{:S(2)}, u32[]{:S(2)}) collective-permute-start(bf16[64,24,128]{2,1,0:T(8,128)(2,1)S(1)} %get-tuple-element.13), channel_id=1, source_target_pairs={{0,16},{16,0},{128,144},{144,128},{1,17},{17,1},{129,145},{145,129... | collective-permute-start | bytes 1179656 | tf_op jit(solution)/shard_map/ppermute | solution.py:240
  52.0 6.5 %all-to-all-start.1 = ((bf16[64,32,128]{2,1,0:T(8,128)(2,1)}), bf16[64,32,128]{2,1,0:T(8,128)(2,1)S(1)}, u32[]{:S(2)}, u32[]{:S(2)}) async-start(bf16[64,32,128]{2,1,0:T(8,128)(2,1)} %pad_maximum_fusion), calls=%async_computation.1 | async-start | bytes 1048576 | tf_op jit(solution)/shard_map/all_to_all | solution.py:251
  58.5 0.1 pad_add_fusion.where
  58.6 0.2 collective-permute-start.5
  58.8 2.6 %collective-permute-done.4.source = bf16[64,24,128]{2,1,0:T(8,128)(2,1)S(1)} collective-permute-done((bf16[64,24,128]{2,1,0:T(8,128)(2,1)S(1)}, bf16[64,24,128]{2,1,0:T(8,128)(2,1)S(1)}, u32[]{:S(2)}, u32[]{:S(2)}) %collective-permute-start.4) | collective-permute-done | bytes 393248 | tf_op jit(solution)/shard_map/ppermute | solution.py:240
  61.4 0.1 shard_map.48.far
  61.4 8.6 %collective-permute-done.6.both = bf16[64,24,128]{2,1,0:T(8,128)(2,1)S(1)} collective-permute-done((bf16[64,24,128]{2,1,0:T(8,128)(2,1)S(1)}, bf16[64,24,128]{2,1,0:T(8,128)(2,1)S(1)}, u32[]{:S(2)}, u32[]{:S(2)}) %collective-permute-start.6) | collective-permute-done | bytes 393248 | tf_op jit(solution)/shard_map/ppermute | solution.py:240
  70.0 5.8 %all-to-all-done.1.small = bf16[64,32,128]{2,1,0:T(8,128)(2,1)S(1)} async-done(((bf16[64,32,128]{2,1,0:T(8,128)(2,1)}), bf16[64,32,128]{2,1,0:T(8,128)(2,1)S(1)}, u32[]{:S(2)}, u32[]{:S(2)}) %all-to-all-start.1) | async-done | bytes 524320 | tf_op jit(solution)/shard_map/all_to_all | solution.py:251
  75.8 5.9 %shard_map.49 = f32[2,1,512,1024]{3,2,1,0:T(8,128)} custom-call(s32[2]{0:T(128)S(1)} %pad_add_fusion.where, bf16[64,24,128]{2,1,0:T(8,128)(2,1)S(1)} %get-tuple-element.14.mine, bf16[1536,128]{1,0:T(8,128)(2,1)S(1)} %shard_map.48.far, bf16[64,24,128]{2,1,0:T(8,128)(2,1)S(1)} %collective-permute-done.5.near, ...), custom_call_target="tpu_custom_call" | custom-call | flops 2147483648 | bytes 7340032 | tf_op jit(solution)/shard_map/pallas_call | solution.py:219
  (4 shorter events, 0.0 us)
Async XLA Ops:
  9.8 16.6 %collective-permute-start = (bf16[4,8,2048]{2,1,0:T(8,128)(2,1)}, bf16[4,8,2048]{2,1,0:T(8,128)(2,1)S(1)}, u32[]{:S(2)}, u32[]{:S(2)}) collective-permute-start(bf16[4,8,2048]{2,1,0:T(8,128)(2,1)} %get-tuple-element.10), channel_id=1, source_target_pairs={{0,128},{1,129},{2,130},{3,131},{4,132},{5,133},{6,134},{7,135},{8... | collective-permute-start | bytes 393224 | tf_op jit(solution)/shard_map/ppermute | solution.py:276
  13.8 35.6 %all-to-all-start = ((bf16[64,2,24,128]{3,2,1,0:T(8,128)(2,1)}), bf16[64,2,24,128]{3,2,1,0:T(8,128)(2,1)S(1)}, u32[]{:S(2)}, u32[]{:S(2)}) async-start(bf16[64,2,24,128]{3,2,1,0:T(8,128)(2,1)} %bitcast.15), calls=%async_computation | async-start | bytes 1572864 | tf_op jit(solution)/shard_map/all_to_all | solution.py:251
  26.4 0.7 copy-start
  33.3 4.7 %collective-permute-start.2 = (bf16[64,8,128]{2,1,0:T(8,128)(2,1)S(1)}, bf16[64,8,128]{2,1,0:T(8,128)(2,1)S(1)}, u32[]{:S(2)}, u32[]{:S(2)}) collective-permute-start(bf16[64,8,128]{2,1,0:T(8,128)(2,1)S(1)} %get-tuple-element.15), channel_id=1, source_target_pairs={{0,128},{16,144},{128,0},{144,16},{1,129},{17,145},{129,1},{145,17... | collective-permute-start | bytes 393224 | tf_op jit(solution)/shard_map/ppermute | solution.py:240
  33.4 7.9 %collective-permute-start.3 = (bf16[64,8,128]{2,1,0:T(8,128)(2,1)S(1)}, bf16[64,8,128]{2,1,0:T(8,128)(2,1)S(1)}, u32[]{:S(2)}, u32[]{:S(2)}) collective-permute-start(bf16[64,8,128]{2,1,0:T(8,128)(2,1)S(1)} %get-tuple-element.16), channel_id=1, source_target_pairs={{0,144},{16,128},{128,16},{144,0},{1,145},{17,129},{129,17},{145,1... | collective-permute-start | bytes 393224 | tf_op jit(solution)/shard_map/ppermute | solution.py:240
  36.1 5.6 %collective-permute-start.1 = (bf16[64,8,128]{2,1,0:T(8,128)(2,1)S(1)}, bf16[64,8,128]{2,1,0:T(8,128)(2,1)S(1)}, u32[]{:S(2)}, u32[]{:S(2)}) collective-permute-start(bf16[64,8,128]{2,1,0:T(8,128)(2,1)S(1)} %get-tuple-element.16), channel_id=1, source_target_pairs={{0,16},{16,0},{128,144},{144,128},{1,17},{17,1},{129,145},{145,129... | collective-permute-start | bytes 393224 | tf_op jit(solution)/shard_map/ppermute | solution.py:240
  49.5 11.9 %collective-permute-start.4 = (bf16[64,24,128]{2,1,0:T(8,128)(2,1)S(1)}, bf16[64,24,128]{2,1,0:T(8,128)(2,1)S(1)}, u32[]{:S(2)}, u32[]{:S(2)}) collective-permute-start(bf16[64,24,128]{2,1,0:T(8,128)(2,1)S(1)} %get-tuple-element.13), channel_id=1, source_target_pairs={{0,16},{16,0},{128,144},{144,128},{1,17},{17,1},{129,145},{145,129... | collective-permute-start | bytes 1179656 | tf_op jit(solution)/shard_map/ppermute | solution.py:240
  52.0 23.8 %all-to-all-start.1 = ((bf16[64,32,128]{2,1,0:T(8,128)(2,1)}), bf16[64,32,128]{2,1,0:T(8,128)(2,1)S(1)}, u32[]{:S(2)}, u32[]{:S(2)}) async-start(bf16[64,32,128]{2,1,0:T(8,128)(2,1)} %pad_maximum_fusion), calls=%async_computation.1 | async-start | bytes 1048576 | tf_op jit(solution)/shard_map/all_to_all | solution.py:251
  58.5 11.5 %collective-permute-start.6 = (bf16[64,24,128]{2,1,0:T(8,128)(2,1)S(1)}, bf16[64,24,128]{2,1,0:T(8,128)(2,1)S(1)}, u32[]{:S(2)}, u32[]{:S(2)}) collective-permute-start(bf16[64,24,128]{2,1,0:T(8,128)(2,1)S(1)} %get-tuple-element.13), channel_id=1, source_target_pairs={{0,144},{16,128},{128,16},{144,0},{1,145},{17,129},{129,17},{145,1... | collective-permute-start | bytes 1179656 | tf_op jit(solution)/shard_map/ppermute | solution.py:240
  58.6 11.4 %collective-permute-start.5 = (bf16[64,24,128]{2,1,0:T(8,128)(2,1)S(1)}, bf16[64,24,128]{2,1,0:T(8,128)(2,1)S(1)}, u32[]{:S(2)}, u32[]{:S(2)}) collective-permute-start(bf16[64,24,128]{2,1,0:T(8,128)(2,1)S(1)} %get-tuple-element.14.mine), channel_id=1, source_target_pairs={{0,128},{16,144},{128,0},{144,16},{1,129},{17,145},{129,1},{145,17... | collective-permute-start | bytes 1179656 | tf_op jit(solution)/shard_map/ppermute | solution.py:240

commit v5 on v4

--- a/solution.py
+++ b/solution.py
@@ -22,7 +22,7 @@
 PLANE = ("y", "z", "core")
 BANK_FLOPS = 20 * 1024**3
 ROWS_FLOPS = 9 * 1024**3
-COLUMNS = 256
+COLUMNS = 512
 MIB = 1024 * 1024
 VMEM_BANK = 56 * MIB
 VMEM_VIS = 28 * MIB
@@ -45,7 +45,7 @@
 
 
 def filterbank_kernel(first, halo_at, frames, halo, window, table, *refs):
-    out, (held, dft, summed, turned, sem) = refs[0], refs[-5:]
+    out, (held, weight, dft, summed, turned, sem) = refs[0], refs[-6:]
     inputs = held.shape[1]
     count = out.shape[0]
     units = out.shape[1] // inputs
@@ -56,18 +56,21 @@
         return pltpu.make_async_copy(
             frames.at[pl.ds(first + piece * PIECE, PIECE)],
             held.at[pl.ds(HALO + piece * PIECE, PIECE)],
-            sem.at[2 + piece],
+            sem.at[3 + piece],
         )
 
     halo_copy = pltpu.make_async_copy(
         halo.at[pl.ds(halo_at, HALO)], held.at[pl.ds(0, HALO)], sem.at[0]
     )
     table_copy = pltpu.make_async_copy(table, dft, sem.at[1])
+    window_copy = pltpu.make_async_copy(window, weight, sem.at[2])
+    window_copy.start()
     halo_copy.start()
     copy(0).start()
     table_copy.start()
     for piece in range(1, units * pieces):
         copy(piece).start()
+    window_copy.wait()
     halo_copy.wait()
 
     table_copy.wait()
@@ -77,40 +80,43 @@
         for g in range(PIECE // GROUP):
             at = piece * PIECE + g * GROUP + HALO - TAPS + 1
             some = held[pl.ds(at, GROUP + TAPS - 1), :, lanes].astype(F32)
-            total = window[0:1, lanes][None] * some[0:GROUP]
+            total = weight[0:1, lanes][None] * some[0:GROUP]
             for k in range(1, TAPS):
-                total = total + window[k : k + 1, lanes][None] * some[k : k + GROUP]
+                total = total + weight[k : k + 1, lanes][None] * some[k : k + GROUP]
             total = total.reshape(GROUP * inputs, DEPTH)
             high.append(total.astype(BF16))
             rest.append((total - high[-1].astype(F32)).astype(BF16))
         return jnp.concatenate(high + rest, 0)
 
+    def turn(u, i):
+        both = jnp.concatenate(
+            [summed[lax.rem(u, 2), part, pl.ds(i, UNIT, stride=inputs), :] for part in range(2)], 0
+        )
+        turned[pl.ds(u * inputs + i, count, stride=units * inputs), :] = both.T
+
     def body(piece, carry):
         copy(piece).wait()
+        u, step = piece // pieces, lax.rem(piece, pieces)
+        for i in range(inputs // pieces):
+            turn(jnp.maximum(u - 1, 0), step * (inputs // pieces) + i)
         product = None
         for n in range(FRAME // DEPTH):
             lanes = slice(n * DEPTH, (n + 1) * DEPTH)
             term = jnp.dot(split(piece, lanes), dft[lanes, :], preferred_element_type=F32)
             product = term if product is None else product + term
         product = product[:span] + product[span:]
-        row = pl.multiple_of(lax.rem(piece, pieces) * span, span)
+        row = pl.multiple_of(step * span, span)
         for part in range(2):
-            summed[part, pl.ds(row, span), :] = product[:, part * count : (part + 1) * count]
-
-        @pl.when(lax.rem(piece, pieces) == pieces - 1)
-        def _():
-            for i in range(inputs):
-                both = jnp.concatenate(
-                    [summed[part, pl.ds(i, UNIT, stride=inputs), :] for part in range(2)], 0
-                )
-                row = piece // pieces * inputs + i
-                turned[pl.ds(row, count, stride=units * inputs), :] = both.T
-
+            summed[lax.rem(u, 2), part, pl.ds(row, span), :] = product[
+                :, part * count : (part + 1) * count
+            ]
         return carry
 
     lax.fori_loop(0, units * pieces, body, 0)
+    for i in range(inputs):
+        turn(units - 1, i)
     out[...] = turned[...].reshape(count, units * inputs, 2 * UNIT).astype(BF16)
-    for last in refs[1:-5]:
+    for last in refs[1:-6]:
         last[...] = held[units * UNIT :]
 
 
@@ -122,7 +128,7 @@
     here = pl.BlockSpec(memory_space=pltpu.VMEM)
     return pl.pallas_call(
         functools.partial(filterbank_kernel, first, halo_at),
-        in_specs=[there, there, here, there],
+        in_specs=[there] * 4,
         out_specs=[here] * (1 + tail),
         out_shape=[
             jax.ShapeDtypeStruct((count, units * inputs, 2 * UNIT), BF16),
@@ -130,10 +136,11 @@
         ][: 1 + tail],
         scratch_shapes=[
             pltpu.VMEM((HALO + spectra, inputs, FRAME), BF16),
+            pltpu.VMEM(window.shape, F32),
             pltpu.VMEM(table.shape, BF16),
-            pltpu.VMEM((2, UNIT * inputs, count), F32),
+            pltpu.VMEM((2, 2, UNIT * inputs, count), F32),
             pltpu.VMEM((count * units * inputs, 2 * UNIT), F32),
-            pltpu.SemaphoreType.DMA((2 + spectra // PIECE,)),
+            pltpu.SemaphoreType.DMA((3 + spectra // PIECE,)),
         ],
         compiler_params=pltpu.CompilerParams(vmem_limit_bytes=VMEM_BANK),
         cost_estimate=pl.CostEstimate(

time: 82.1 us -> 81.2 us (0.989)
  Pallas kernels: 21 us -> 19.7 us
    pallas_call x2, Pallas kernels: 15 us -> 14 us  [filterbank(): pl.pallas_call(functools.partial(filterbank_kernel, first, halo_at), in_s...]
  transfers between devices with their start and end apart: 9 -> 9, of which waited for: 7 -> 7; matrix products, arithmetic and copies ran while one was open for 2% -> 2% of each run, Pallas kernels for 7% -> 6%
where the time goes in v5:
time: 81.2 us; the launch traced here: 80.8 us
  waiting for transfers between devices  29.2 us (36%)
  starting transfers between devices  29.1 us (36%)
  Pallas kernels  19.7 us (24%)
  local copies, waits for them, and re-layouts  1.75 us (2%)
  other arithmetic  0.96 us (1%)
    all_to_all x2, starting transfers between devices, over_plane(): return lax.all_to_all(array, PLANE, split_axis=0, concat_axis=0, tiled=True)  19.1 us
    ppermute x6, waiting for transfers between devices, swap(): return lax.ppermute(array, ('ta', 'xh'), route)  16.2 us
    pallas_call x2, Pallas kernels, filterbank(): pl.pallas_call(functools.partial(filterbank_kernel, first, halo_at), in_s...  14 us
    all_to_all x2, waiting for transfers between devices, over_plane(): return lax.all_to_all(array, PLANE, split_axis=0, concat_axis=0, tiled=True)  13 us
    ppermute x6, starting transfers between devices, swap(): return lax.ppermute(array, ('ta', 'xh'), route)  6.09 us
    pallas_call x1, Pallas kernels, visibilities(): pl.pallas_call(functools.partial(visibility_kernel, inputs, scale), grid_...  5.57 us
    ppermute x1, starting transfers between devices, local(): earlier = lax.ppermute(last, 'ta', [(i, i + 1) for i in range(n_time - 1)])  3.95 us
  transfers between devices with their start and end apart: 9, of which 7 were waited for; matrix products, arithmetic and copies ran while one was open for 2% of the time, Pallas kernels for 6%

profile of v5, /device:TPU:1, one launch (start us, length us, event | category | flops | bytes accessed | tf_op | source)
XLA Modules:
  0.0 80.8 jit_solution(2774619911798278473)
XLA Ops:
  0.0 9.3 %shard_map.46 = (bf16[128,24,128]{2,1,0:T(8,128)(2,1)}, bf16[4,8,2048]{2,1,0:T(8,128)(2,1)}) custom-call(bf16[256,8,2048]{2,1,0:T(8,128)(2,1)} %bitcast.17, bf16[256,8,2048]{2,1,0:T(8,128)(2,1)} %bitcast.18, f32[4,2048]{1,0:T(4,128)} %constant.34.clone.window, bf16[2048,256]{1,0:T(8,128)(2,1)} %constant.36.clone.table), custom_call_target="tpu_custom_call" | custom-call | flops 21474836480 | bytes 7340032 | tf_op jit(solution)/shard_map/pallas_call | solution.py:129
  9.3 4.0 %collective-permute-start = (bf16[4,8,2048]{2,1,0:T(8,128)(2,1)}, bf16[4,8,2048]{2,1,0:T(8,128)(2,1)S(1)}, u32[]{:S(2)}, u32[]{:S(2)}) collective-permute-start(bf16[4,8,2048]{2,1,0:T(8,128)(2,1)} %get-tuple-element.10), channel_id=1, source_target_pairs={{0,128},{1,129},{2,130},{3,131},{4,132},{5,133},{6,134},{7,135},{8... | collective-permute-start | bytes 393224 | tf_op jit(solution)/shard_map/ppermute | solution.py:283
  13.2 12.6 %all-to-all-start = ((bf16[64,2,24,128]{3,2,1,0:T(8,128)(2,1)}), bf16[64,2,24,128]{3,2,1,0:T(8,128)(2,1)S(1)}, u32[]{:S(2)}, u32[]{:S(2)}) async-start(bf16[64,2,24,128]{3,2,1,0:T(8,128)(2,1)} %bitcast.15), calls=%async_computation | async-start | bytes 1572864 | tf_op jit(solution)/shard_map/all_to_all | solution.py:258
  25.9 0.6 copy-done
  26.5 4.8 %shard_map.47 = bf16[128,8,128]{2,1,0:T(8,128)(2,1)} custom-call(bf16[256,8,2048]{2,1,0:T(8,128)(2,1)} %bitcast.19, bf16[4,8,2048]{2,1,0:T(8,128)(2,1)} %copy-done, f32[4,2048]{1,0:T(4,128)} %constant.34.clone.window, bf16[2048,256]{1,0:T(8,128)(2,1)} %constant.35.clone.table), custom_call_target="tpu_custom_call" | custom-call | flops 21474836480 | bytes 3145728 | tf_op jit(solution)/shard_map/pallas_call | solution.py:129
  31.3 1.0 %dynamic-slice_bitcast_fusion.3 = (bf16[64,8,128]{2,1,0:T(8,128)(2,1)S(1)}, bf16[64,8,128]{2,1,0:T(8,128)(2,1)S(1)}) fusion(bf16[2,64,8,128]{3,2,1,0:T(8,128)(2,1)} %bitcast.16, s32[]{:T(128)S(6)} %select_n.10, s32[]{:T(128)S(6)} %select_n.11), kind=kLoop, calls=%fused_computation.4 | loop fusion | bytes 524296 | tf_op jit(solution)/shard_map/jit(dynamic_index_in_dim)/squeeze | solution.py:263
  32.3 0.1 collective-permute-start.2
  32.4 2.7 %collective-permute-start.3 = (bf16[64,8,128]{2,1,0:T(8,128)(2,1)S(1)}, bf16[64,8,128]{2,1,0:T(8,128)(2,1)S(1)}, u32[]{:S(2)}, u32[]{:S(2)}) collective-permute-start(bf16[64,8,128]{2,1,0:T(8,128)(2,1)S(1)} %get-tuple-element.16), channel_id=1, source_target_pairs={{0,144},{16,128},{128,16},{144,0},{1,145},{17,129},{129,17},{145,1... | collective-permute-start | bytes 393224 | tf_op jit(solution)/shard_map/ppermute | solution.py:247
  35.1 0.5 collective-permute-start.1
  35.6 1.4 %collective-permute-done.2 = bf16[64,8,128]{2,1,0:T(8,128)(2,1)S(1)} collective-permute-done((bf16[64,8,128]{2,1,0:T(8,128)(2,1)S(1)}, bf16[64,8,128]{2,1,0:T(8,128)(2,1)S(1)}, u32[]{:S(2)}, u32[]{:S(2)}) %collective-permute-start.2) | collective-permute-done | bytes 131104 | tf_op jit(solution)/shard_map/ppermute | solution.py:247
  37.0 3.3 %collective-permute-done.3 = bf16[64,8,128]{2,1,0:T(8,128)(2,1)S(1)} collective-permute-done((bf16[64,8,128]{2,1,0:T(8,128)(2,1)S(1)}, bf16[64,8,128]{2,1,0:T(8,128)(2,1)S(1)}, u32[]{:S(2)}, u32[]{:S(2)}) %collective-permute-start.3) | collective-permute-done | bytes 131104 | tf_op jit(solution)/shard_map/ppermute | solution.py:247
  40.3 0.4 collective-permute-done.1
  40.7 0.9 %pad_maximum_fusion = bf16[64,32,128]{2,1,0:T(8,128)(2,1)} fusion(bf16[64,8,128]{2,1,0:T(8,128)(2,1)S(1)} %collective-permute-done.3, bf16[64,8,128]{2,1,0:T(8,128)(2,1)S(1)} %collective-permute-done.2, bf16[64,8,128]{2,1,0:T(8,128)(2,1)S(1)} %collective-permute-done.1, bf16[64,8,128]{2,1,0:T(8,128)(2,1)S(1)} %get-tuple-element.15), kind=kLoop, calls=%fused_computation | loop fusion | flops 2097152 | bytes 1048576 | tf_op jit(solution)/shard_map/concatenate | solution.py:286
  41.6 7.2 %all-to-all-done = bf16[64,2,24,128]{3,2,1,0:T(8,128)(2,1)S(1)} async-done(((bf16[64,2,24,128]{3,2,1,0:T(8,128)(2,1)}), bf16[64,2,24,128]{3,2,1,0:T(8,128)(2,1)S(1)}, u32[]{:S(2)}, u32[]{:S(2)}) %all-to-all-start) | async-done | bytes 786464 | tf_op jit(solution)/shard_map/all_to_all | solution.py:258
  48.9 0.1 dynamic-slice_bitcast_fusion
  49.0 2.5 %collective-permute-start.4 = (bf16[64,24,128]{2,1,0:T(8,128)(2,1)S(1)}, bf16[64,24,128]{2,1,0:T(8,128)(2,1)S(1)}, u32[]{:S(2)}, u32[]{:S(2)}) collective-permute-start(bf16[64,24,128]{2,1,0:T(8,128)(2,1)S(1)} %get-tuple-element.13), channel_id=1, source_target_pairs={{0,16},{16,0},{128,144},{144,128},{1,17},{17,1},{129,145},{145,129... | collective-permute-start | bytes 1179656 | tf_op jit(solution)/shard_map/ppermute | solution.py:247
  51.5 6.5 %all-to-all-start.1 = ((bf16[64,32,128]{2,1,0:T(8,128)(2,1)}), bf16[64,32,128]{2,1,0:T(8,128)(2,1)S(1)}, u32[]{:S(2)}, u32[]{:S(2)}) async-start(bf16[64,32,128]{2,1,0:T(8,128)(2,1)} %pad_maximum_fusion), calls=%async_computation.1 | async-start | bytes 1048576 | tf_op jit(solution)/shard_map/all_to_all | solution.py:258
  58.0 0.1 pad_add_fusion.where
  58.1 0.2 collective-permute-start.5
  58.3 2.6 %collective-permute-done.4.source = bf16[64,24,128]{2,1,0:T(8,128)(2,1)S(1)} collective-permute-done((bf16[64,24,128]{2,1,0:T(8,128)(2,1)S(1)}, bf16[64,24,128]{2,1,0:T(8,128)(2,1)S(1)}, u32[]{:S(2)}, u32[]{:S(2)}) %collective-permute-start.4) | collective-permute-done | bytes 393248 | tf_op jit(solution)/shard_map/ppermute | solution.py:247
  60.9 0.1 shard_map.48.far
  60.9 8.6 %collective-permute-done.6.both = bf16[64,24,128]{2,1,0:T(8,128)(2,1)S(1)} collective-permute-done((bf16[64,24,128]{2,1,0:T(8,128)(2,1)S(1)}, bf16[64,24,128]{2,1,0:T(8,128)(2,1)S(1)}, u32[]{:S(2)}, u32[]{:S(2)}) %collective-permute-start.6) | collective-permute-done | bytes 393248 | tf_op jit(solution)/shard_map/ppermute | solution.py:247
  69.5 5.8 %all-to-all-done.1.small = bf16[64,32,128]{2,1,0:T(8,128)(2,1)S(1)} async-done(((bf16[64,32,128]{2,1,0:T(8,128)(2,1)}), bf16[64,32,128]{2,1,0:T(8,128)(2,1)S(1)}, u32[]{:S(2)}, u32[]{:S(2)}) %all-to-all-start.1) | async-done | bytes 524320 | tf_op jit(solution)/shard_map/all_to_all | solution.py:258
  75.3 5.6 %shard_map.49 = f32[2,1,512,1024]{3,2,1,0:T(8,128)} custom-call(s32[2]{0:T(128)S(1)} %pad_add_fusion.where, bf16[64,24,128]{2,1,0:T(8,128)(2,1)S(1)} %get-tuple-element.14.mine, bf16[1536,128]{1,0:T(8,128)(2,1)S(1)} %shard_map.48.far, bf16[64,24,128]{2,1,0:T(8,128)(2,1)S(1)} %collective-permute-done.5.near, ...), custom_call_target="tpu_custom_call" | custom-call | flops 2147483648 | bytes 7340032 | tf_op jit(solution)/shard_map/pallas_call | solution.py:226
  (4 shorter events, 0.0 us)
Async XLA Ops:
  9.3 16.6 %collective-permute-start = (bf16[4,8,2048]{2,1,0:T(8,128)(2,1)}, bf16[4,8,2048]{2,1,0:T(8,128)(2,1)S(1)}, u32[]{:S(2)}, u32[]{:S(2)}) collective-permute-start(bf16[4,8,2048]{2,1,0:T(8,128)(2,1)} %get-tuple-element.10), channel_id=1, source_target_pairs={{0,128},{1,129},{2,130},{3,131},{4,132},{5,133},{6,134},{7,135},{8... | collective-permute-start | bytes 393224 | tf_op jit(solution)/shard_map/ppermute | solution.py:283
  13.2 35.6 %all-to-all-start = ((bf16[64,2,24,128]{3,2,1,0:T(8,128)(2,1)}), bf16[64,2,24,128]{3,2,1,0:T(8,128)(2,1)S(1)}, u32[]{:S(2)}, u32[]{:S(2)}) async-start(bf16[64,2,24,128]{3,2,1,0:T(8,128)(2,1)} %bitcast.15), calls=%async_computation | async-start | bytes 1572864 | tf_op jit(solution)/shard_map/all_to_all | solution.py:258
  25.9 0.7 copy-start
  32.3 4.7 %collective-permute-start.2 = (bf16[64,8,128]{2,1,0:T(8,128)(2,1)S(1)}, bf16[64,8,128]{2,1,0:T(8,128)(2,1)S(1)}, u32[]{:S(2)}, u32[]{:S(2)}) collective-permute-start(bf16[64,8,128]{2,1,0:T(8,128)(2,1)S(1)} %get-tuple-element.15), channel_id=1, source_target_pairs={{0,128},{16,144},{128,0},{144,16},{1,129},{17,145},{129,1},{145,17... | collective-permute-start | bytes 393224 | tf_op jit(solution)/shard_map/ppermute | solution.py:247
  32.4 7.9 %collective-permute-start.3 = (bf16[64,8,128]{2,1,0:T(8,128)(2,1)S(1)}, bf16[64,8,128]{2,1,0:T(8,128)(2,1)S(1)}, u32[]{:S(2)}, u32[]{:S(2)}) collective-permute-start(bf16[64,8,128]{2,1,0:T(8,128)(2,1)S(1)} %get-tuple-element.16), channel_id=1, source_target_pairs={{0,144},{16,128},{128,16},{144,0},{1,145},{17,129},{129,17},{145,1... | collective-permute-start | bytes 393224 | tf_op jit(solution)/shard_map/ppermute | solution.py:247
  35.1 5.6 %collective-permute-start.1 = (bf16[64,8,128]{2,1,0:T(8,128)(2,1)S(1)}, bf16[64,8,128]{2,1,0:T(8,128)(2,1)S(1)}, u32[]{:S(2)}, u32[]{:S(2)}) collective-permute-start(bf16[64,8,128]{2,1,0:T(8,128)(2,1)S(1)} %get-tuple-element.16), channel_id=1, source_target_pairs={{0,16},{16,0},{128,144},{144,128},{1,17},{17,1},{129,145},{145,129... | collective-permute-start | bytes 393224 | tf_op jit(solution)/shard_map/ppermute | solution.py:247
  49.0 11.9 %collective-permute-start.4 = (bf16[64,24,128]{2,1,0:T(8,128)(2,1)S(1)}, bf16[64,24,128]{2,1,0:T(8,128)(2,1)S(1)}, u32[]{:S(2)}, u32[]{:S(2)}) collective-permute-start(bf16[64,24,128]{2,1,0:T(8,128)(2,1)S(1)} %get-tuple-element.13), channel_id=1, source_target_pairs={{0,16},{16,0},{128,144},{144,128},{1,17},{17,1},{129,145},{145,129... | collective-permute-start | bytes 1179656 | tf_op jit(solution)/shard_map/ppermute | solution.py:247
  51.5 23.8 %all-to-all-start.1 = ((bf16[64,32,128]{2,1,0:T(8,128)(2,1)}), bf16[64,32,128]{2,1,0:T(8,128)(2,1)S(1)}, u32[]{:S(2)}, u32[]{:S(2)}) async-start(bf16[64,32,128]{2,1,0:T(8,128)(2,1)} %pad_maximum_fusion), calls=%async_computation.1 | async-start | bytes 1048576 | tf_op jit(solution)/shard_map/all_to_all | solution.py:258
  58.0 11.5 %collective-permute-start.6 = (bf16[64,24,128]{2,1,0:T(8,128)(2,1)S(1)}, bf16[64,24,128]{2,1,0:T(8,128)(2,1)S(1)}, u32[]{:S(2)}, u32[]{:S(2)}) collective-permute-start(bf16[64,24,128]{2,1,0:T(8,128)(2,1)S(1)} %get-tuple-element.13), channel_id=1, source_target_pairs={{0,144},{16,128},{128,16},{144,0},{1,145},{17,129},{129,17},{145,1... | collective-permute-start | bytes 1179656 | tf_op jit(solution)/shard_map/ppermute | solution.py:247
  58.1 11.4 %collective-permute-start.5 = (bf16[64,24,128]{2,1,0:T(8,128)(2,1)S(1)}, bf16[64,24,128]{2,1,0:T(8,128)(2,1)S(1)}, u32[]{:S(2)}, u32[]{:S(2)}) collective-permute-start(bf16[64,24,128]{2,1,0:T(8,128)(2,1)S(1)} %get-tuple-element.14.mine), channel_id=1, source_target_pairs={{0,128},{16,144},{128,0},{144,16},{1,129},{17,145},{129,1},{145,17... | collective-permute-start | bytes 1179656 | tf_op jit(solution)/shard_map/ppermute | solution.py:247

commit v6 on v5

--- a/solution.py
+++ b/solution.py
@@ -280,7 +280,8 @@
         frames, start, spectra - start, frames, start - HALO, window, x_last, True
     )
     turned_late = over_plane(late.reshape(n_plane, 2, *late.shape[1:]))
-    earlier = lax.ppermute(last, "ta", [(i, i + 1) for i in range(n_time - 1)])
+    earlier = lax.ppermute(last, "ta", [(i, (i + 1) % n_time) for i in range(n_time)])
+    earlier = jnp.where(lax.axis_index("ta") == 0, jnp.zeros_like(earlier), earlier)
     (early,) = filterbank(frames, 0, start, earlier, 0, window, x_first, False)
     sources_early = along_x(*by_x(early.reshape(2, n_plane, *early.shape[1:]), 0))
     stacked = jnp.concatenate(sources_early, 1)

time: 81.2 us -> 79.3 us (0.977)
  starting transfers between devices: 29.1 us -> 27.3 us
    ppermute x1, starting transfers between devices: 3.95 us -> 2.13 us  [local(): lax.ppermute(last, 'ta', [(i, (i + 1) % n_time) for i in range(n_time)])]
  transfers between devices with their start and end apart: 9 -> 9, of which waited for: 7 -> 7; matrix products, arithmetic and copies ran while one was open for 2% -> 3% of each run, Pallas kernels for 6% -> 6%
where the time goes in v6:
time: 79.3 us; the launch traced here: 79 us
  waiting for transfers between devices  29.2 us (37%)
  starting transfers between devices  27.3 us (34%)
  Pallas kernels  19.7 us (25%)
  other arithmetic  1.63 us (2%)
  local copies, waits for them, and re-layouts  1.11 us (1%)
    all_to_all x2, starting transfers between devices, over_plane(): return lax.all_to_all(array, PLANE, split_axis=0, concat_axis=0, tiled=True)  19.1 us
    ppermute x6, waiting for transfers between devices, swap(): return lax.ppermute(array, ('ta', 'xh'), route)  16.3 us
    pallas_call x2, Pallas kernels, filterbank(): pl.pallas_call(functools.partial(filterbank_kernel, first, halo_at), in_s...  14 us
    all_to_all x2, waiting for transfers between devices, over_plane(): return lax.all_to_all(array, PLANE, split_axis=0, concat_axis=0, tiled=True)  12.9 us
    ppermute x6, starting transfers between devices, swap(): return lax.ppermute(array, ('ta', 'xh'), route)  6.11 us
    pallas_call x1, Pallas kernels, visibilities(): pl.pallas_call(functools.partial(visibility_kernel, inputs, scale), grid_...  5.57 us
    ppermute x1, starting transfers between devices, local(): lax.ppermute(last, 'ta', [(i, (i + 1) % n_time) for i in range(n_time)])  2.13 us
  transfers between devices with their start and end apart: 9, of which 7 were waited for; matrix products, arithmetic and copies ran while one was open for 3% of the time, Pallas kernels for 6%

profile of v6, /device:TPU:1, one launch (start us, length us, event | category | flops | bytes accessed | tf_op | source)
XLA Modules:
  0.0 79.0 jit_solution(3587634136992223916)
XLA Ops:
  0.0 9.3 %shard_map.46 = (bf16[128,24,128]{2,1,0:T(8,128)(2,1)}, bf16[4,8,2048]{2,1,0:T(8,128)(2,1)}) custom-call(bf16[256,8,2048]{2,1,0:T(8,128)(2,1)} %bitcast.17, bf16[256,8,2048]{2,1,0:T(8,128)(2,1)} %bitcast.18, f32[4,2048]{1,0:T(4,128)} %constant.37.clone.window, bf16[2048,256]{1,0:T(8,128)(2,1)} %constant.39.clone.table), custom_call_target="tpu_custom_call" | custom-call | flops 21474836480 | bytes 7340032 | tf_op jit(solution)/shard_map/pallas_call | solution.py:129
  9.3 2.1 %collective-permute-start = (bf16[4,8,2048]{2,1,0:T(8,128)(2,1)}, bf16[4,8,2048]{2,1,0:T(8,128)(2,1)S(1)}, u32[]{:S(2)}, u32[]{:S(2)}) collective-permute-start(bf16[4,8,2048]{2,1,0:T(8,128)(2,1)} %get-tuple-element.10), channel_id=1, source_target_pairs={{0,128},{128,0},{1,129},{129,1},{2,130},{130,2},{3,131},{131,3},{4... | collective-permute-start | bytes 393224 | tf_op jit(solution)/shard_map/ppermute | solution.py:283
  11.4 12.6 %all-to-all-start = ((bf16[64,2,24,128]{3,2,1,0:T(8,128)(2,1)}), bf16[64,2,24,128]{3,2,1,0:T(8,128)(2,1)S(1)}, u32[]{:S(2)}, u32[]{:S(2)}) async-start(bf16[64,2,24,128]{3,2,1,0:T(8,128)(2,1)} %bitcast.15), calls=%async_computation | async-start | bytes 1572864 | tf_op jit(solution)/shard_map/all_to_all | solution.py:258
  24.0 0.7 broadcast_select_fusion.halo
  24.7 4.7 %shard_map.47 = bf16[128,8,128]{2,1,0:T(8,128)(2,1)} custom-call(bf16[256,8,2048]{2,1,0:T(8,128)(2,1)} %bitcast.19, bf16[4,8,2048]{2,1,0:T(8,128)(2,1)} %broadcast_select_fusion.halo, f32[4,2048]{1,0:T(4,128)} %constant.37.clone.window, bf16[2048,256]{1,0:T(8,128)(2,1)} %constant.38.clone.table), custom_call_target="tpu_custom_call" | custom-call | flops 21474836480 | bytes 3145728 | tf_op jit(solution)/shard_map/pallas_call | solution.py:129
  29.5 1.0 %dynamic-slice_bitcast_fusion.3 = (bf16[64,8,128]{2,1,0:T(8,128)(2,1)S(1)}, bf16[64,8,128]{2,1,0:T(8,128)(2,1)S(1)}) fusion(bf16[2,64,8,128]{3,2,1,0:T(8,128)(2,1)} %bitcast.16, s32[]{:T(128)S(6)} %select_n.20, s32[]{:T(128)S(6)} %select_n.21), kind=kLoop, calls=%fused_computation.4 | loop fusion | bytes 524296 | tf_op jit(solution)/shard_map/jit(dynamic_index_in_dim)/squeeze | solution.py:263
  30.5 0.3 collective-permute-start.2
  30.8 2.5 %collective-permute-start.3 = (bf16[64,8,128]{2,1,0:T(8,128)(2,1)S(1)}, bf16[64,8,128]{2,1,0:T(8,128)(2,1)S(1)}, u32[]{:S(2)}, u32[]{:S(2)}) collective-permute-start(bf16[64,8,128]{2,1,0:T(8,128)(2,1)S(1)} %get-tuple-element.16), channel_id=1, source_target_pairs={{0,144},{16,128},{128,16},{144,0},{1,145},{17,129},{129,17},{145,1... | collective-permute-start | bytes 393224 | tf_op jit(solution)/shard_map/ppermute | solution.py:247
  33.3 0.5 collective-permute-start.1
  33.8 1.4 %collective-permute-done.2 = bf16[64,8,128]{2,1,0:T(8,128)(2,1)S(1)} collective-permute-done((bf16[64,8,128]{2,1,0:T(8,128)(2,1)S(1)}, bf16[64,8,128]{2,1,0:T(8,128)(2,1)S(1)}, u32[]{:S(2)}, u32[]{:S(2)}) %collective-permute-start.2) | collective-permute-done | bytes 131104 | tf_op jit(solution)/shard_map/ppermute | solution.py:247
  35.2 3.2 %collective-permute-done.3 = bf16[64,8,128]{2,1,0:T(8,128)(2,1)S(1)} collective-permute-done((bf16[64,8,128]{2,1,0:T(8,128)(2,1)S(1)}, bf16[64,8,128]{2,1,0:T(8,128)(2,1)S(1)}, u32[]{:S(2)}, u32[]{:S(2)}) %collective-permute-start.3) | collective-permute-done | bytes 131104 | tf_op jit(solution)/shard_map/ppermute | solution.py:247
  38.4 0.6 collective-permute-done.1
  39.0 0.9 %pad_maximum_fusion = bf16[64,32,128]{2,1,0:T(8,128)(2,1)} fusion(bf16[64,8,128]{2,1,0:T(8,128)(2,1)S(1)} %collective-permute-done.3, bf16[64,8,128]{2,1,0:T(8,128)(2,1)S(1)} %collective-permute-done.2, bf16[64,8,128]{2,1,0:T(8,128)(2,1)S(1)} %collective-permute-done.1, bf16[64,8,128]{2,1,0:T(8,128)(2,1)S(1)} %get-tuple-element.15), kind=kLoop, calls=%fused_computation | loop fusion | flops 2097152 | bytes 1048576 | tf_op jit(solution)/shard_map/concatenate | solution.py:287
  39.9 7.1 %all-to-all-done = bf16[64,2,24,128]{3,2,1,0:T(8,128)(2,1)S(1)} async-done(((bf16[64,2,24,128]{3,2,1,0:T(8,128)(2,1)}), bf16[64,2,24,128]{3,2,1,0:T(8,128)(2,1)S(1)}, u32[]{:S(2)}, u32[]{:S(2)}) %all-to-all-start) | async-done | bytes 786464 | tf_op jit(solution)/shard_map/all_to_all | solution.py:258
  47.0 0.1 dynamic-slice_bitcast_fusion
  47.1 2.5 %collective-permute-start.4 = (bf16[64,24,128]{2,1,0:T(8,128)(2,1)S(1)}, bf16[64,24,128]{2,1,0:T(8,128)(2,1)S(1)}, u32[]{:S(2)}, u32[]{:S(2)}) collective-permute-start(bf16[64,24,128]{2,1,0:T(8,128)(2,1)S(1)} %get-tuple-element.13), channel_id=1, source_target_pairs={{0,16},{16,0},{128,144},{144,128},{1,17},{17,1},{129,145},{145,129... | collective-permute-start | bytes 1179656 | tf_op jit(solution)/shard_map/ppermute | solution.py:247
  49.6 6.5 %all-to-all-start.1 = ((bf16[64,32,128]{2,1,0:T(8,128)(2,1)}), bf16[64,32,128]{2,1,0:T(8,128)(2,1)S(1)}, u32[]{:S(2)}, u32[]{:S(2)}) async-start(bf16[64,32,128]{2,1,0:T(8,128)(2,1)} %pad_maximum_fusion), calls=%async_computation.1 | async-start | bytes 1048576 | tf_op jit(solution)/shard_map/all_to_all | solution.py:258
  56.1 0.1 pad_add_fusion.where
  56.2 0.3 collective-permute-start.6
  56.5 2.6 %collective-permute-done.4.source = bf16[64,24,128]{2,1,0:T(8,128)(2,1)S(1)} collective-permute-done((bf16[64,24,128]{2,1,0:T(8,128)(2,1)S(1)}, bf16[64,24,128]{2,1,0:T(8,128)(2,1)S(1)}, u32[]{:S(2)}, u32[]{:S(2)}) %collective-permute-start.4) | collective-permute-done | bytes 393248 | tf_op jit(solution)/shard_map/ppermute | solution.py:247
  59.0 0.1 shard_map.48.far
  59.1 8.6 %collective-permute-done.6.both = bf16[64,24,128]{2,1,0:T(8,128)(2,1)S(1)} collective-permute-done((bf16[64,24,128]{2,1,0:T(8,128)(2,1)S(1)}, bf16[64,24,128]{2,1,0:T(8,128)(2,1)S(1)}, u32[]{:S(2)}, u32[]{:S(2)}) %collective-permute-start.6) | collective-permute-done | bytes 393248 | tf_op jit(solution)/shard_map/ppermute | solution.py:247
  67.7 5.8 %all-to-all-done.1.small = bf16[64,32,128]{2,1,0:T(8,128)(2,1)S(1)} async-done(((bf16[64,32,128]{2,1,0:T(8,128)(2,1)}), bf16[64,32,128]{2,1,0:T(8,128)(2,1)S(1)}, u32[]{:S(2)}, u32[]{:S(2)}) %all-to-all-start.1) | async-done | bytes 524320 | tf_op jit(solution)/shard_map/all_to_all | solution.py:258
  73.4 5.6 %shard_map.49 = f32[2,1,512,1024]{3,2,1,0:T(8,128)} custom-call(s32[2]{0:T(128)S(1)} %pad_add_fusion.where, bf16[64,24,128]{2,1,0:T(8,128)(2,1)S(1)} %get-tuple-element.14.mine, bf16[1536,128]{1,0:T(8,128)(2,1)S(1)} %shard_map.48.far, bf16[64,24,128]{2,1,0:T(8,128)(2,1)S(1)} %collective-permute-done.5.near, ...), custom_call_target="tpu_custom_call" | custom-call | flops 2147483648 | bytes 7340032 | tf_op jit(solution)/shard_map/pallas_call | solution.py:226
  (3 shorter events, 0.0 us)
Async XLA Ops:
  9.3 14.8 %collective-permute-start = (bf16[4,8,2048]{2,1,0:T(8,128)(2,1)}, bf16[4,8,2048]{2,1,0:T(8,128)(2,1)S(1)}, u32[]{:S(2)}, u32[]{:S(2)}) collective-permute-start(bf16[4,8,2048]{2,1,0:T(8,128)(2,1)} %get-tuple-element.10), channel_id=1, source_target_pairs={{0,128},{128,0},{1,129},{129,1},{2,130},{130,2},{3,131},{131,3},{4... | collective-permute-start | bytes 393224 | tf_op jit(solution)/shard_map/ppermute | solution.py:283
  11.4 35.6 %all-to-all-start = ((bf16[64,2,24,128]{3,2,1,0:T(8,128)(2,1)}), bf16[64,2,24,128]{3,2,1,0:T(8,128)(2,1)S(1)}, u32[]{:S(2)}, u32[]{:S(2)}) async-start(bf16[64,2,24,128]{3,2,1,0:T(8,128)(2,1)} %bitcast.15), calls=%async_computation | async-start | bytes 1572864 | tf_op jit(solution)/shard_map/all_to_all | solution.py:258
  30.5 4.7 %collective-permute-start.2 = (bf16[64,8,128]{2,1,0:T(8,128)(2,1)S(1)}, bf16[64,8,128]{2,1,0:T(8,128)(2,1)S(1)}, u32[]{:S(2)}, u32[]{:S(2)}) collective-permute-start(bf16[64,8,128]{2,1,0:T(8,128)(2,1)S(1)} %get-tuple-element.15), channel_id=1, source_target_pairs={{0,128},{16,144},{128,0},{144,16},{1,129},{17,145},{129,1},{145,17... | collective-permute-start | bytes 393224 | tf_op jit(solution)/shard_map/ppermute | solution.py:247
  30.8 7.6 %collective-permute-start.3 = (bf16[64,8,128]{2,1,0:T(8,128)(2,1)S(1)}, bf16[64,8,128]{2,1,0:T(8,128)(2,1)S(1)}, u32[]{:S(2)}, u32[]{:S(2)}) collective-permute-start(bf16[64,8,128]{2,1,0:T(8,128)(2,1)S(1)} %get-tuple-element.16), channel_id=1, source_target_pairs={{0,144},{16,128},{128,16},{144,0},{1,145},{17,129},{129,17},{145,1... | collective-permute-start | bytes 393224 | tf_op jit(solution)/shard_map/ppermute | solution.py:247
  33.3 5.7 %collective-permute-start.1 = (bf16[64,8,128]{2,1,0:T(8,128)(2,1)S(1)}, bf16[64,8,128]{2,1,0:T(8,128)(2,1)S(1)}, u32[]{:S(2)}, u32[]{:S(2)}) collective-permute-start(bf16[64,8,128]{2,1,0:T(8,128)(2,1)S(1)} %get-tuple-element.16), channel_id=1, source_target_pairs={{0,16},{16,0},{128,144},{144,128},{1,17},{17,1},{129,145},{145,129... | collective-permute-start | bytes 393224 | tf_op jit(solution)/shard_map/ppermute | solution.py:247
  47.1 11.9 %collective-permute-start.4 = (bf16[64,24,128]{2,1,0:T(8,128)(2,1)S(1)}, bf16[64,24,128]{2,1,0:T(8,128)(2,1)S(1)}, u32[]{:S(2)}, u32[]{:S(2)}) collective-permute-start(bf16[64,24,128]{2,1,0:T(8,128)(2,1)S(1)} %get-tuple-element.13), channel_id=1, source_target_pairs={{0,16},{16,0},{128,144},{144,128},{1,17},{17,1},{129,145},{145,129... | collective-permute-start | bytes 1179656 | tf_op jit(solution)/shard_map/ppermute | solution.py:247
  49.6 23.8 %all-to-all-start.1 = ((bf16[64,32,128]{2,1,0:T(8,128)(2,1)}), bf16[64,32,128]{2,1,0:T(8,128)(2,1)S(1)}, u32[]{:S(2)}, u32[]{:S(2)}) async-start(bf16[64,32,128]{2,1,0:T(8,128)(2,1)} %pad_maximum_fusion), calls=%async_computation.1 | async-start | bytes 1048576 | tf_op jit(solution)/shard_map/all_to_all | solution.py:258
  56.2 11.5 %collective-permute-start.6 = (bf16[64,24,128]{2,1,0:T(8,128)(2,1)S(1)}, bf16[64,24,128]{2,1,0:T(8,128)(2,1)S(1)}, u32[]{:S(2)}, u32[]{:S(2)}) collective-permute-start(bf16[64,24,128]{2,1,0:T(8,128)(2,1)S(1)} %get-tuple-element.13), channel_id=1, source_target_pairs={{0,144},{16,128},{128,16},{144,0},{1,145},{17,129},{129,17},{145,1... | collective-permute-start | bytes 1179656 | tf_op jit(solution)/shard_map/ppermute | solution.py:247
  56.5 11.2 %collective-permute-start.5 = (bf16[64,24,128]{2,1,0:T(8,128)(2,1)S(1)}, bf16[64,24,128]{2,1,0:T(8,128)(2,1)S(1)}, u32[]{:S(2)}, u32[]{:S(2)}) collective-permute-start(bf16[64,24,128]{2,1,0:T(8,128)(2,1)S(1)} %get-tuple-element.14.mine), channel_id=1, source_target_pairs={{0,128},{16,144},{128,0},{144,16},{1,129},{17,145},{129,1},{145,17... | collective-permute-start | bytes 1179656 | tf_op jit(solution)/shard_map/ppermute | solution.py:247

commit v7 on v6

--- a/solution.py
+++ b/solution.py
@@ -173,10 +173,10 @@
     )(source)
 
 
-def visibility_kernel(inputs, scale, where, mine, far, near, both, small, out, right, left):
+def visibility_kernel(inputs, scale, where, mine, far, near, both, small, out, right, left, ready, sem):
     groups = mine.shape[0]
     units = mine.shape[1] // inputs
-    n_rows = left.shape[0] // 2
+    n_rows = left.shape[0]
     stripe = groups // N_Y * inputs
     n_lanes = 2 * UNIT
 
@@ -189,34 +189,41 @@
                 y * stripe : (y + 1) * stripe
             ]
 
-    @pl.when(pl.program_id(0) == 0)
-    def _():
-        for origin, source in ((0, mine), (2, near), (3, both)):
-            wide = source[...].astype(F32).reshape(groups, units, inputs, n_lanes)
-            for u in range(units):
-                place(wide[:, u].reshape(groups * inputs, n_lanes).astype(BF16), origin, u)
+    for origin, source in ((0, mine), (2, near), (3, both)):
+        wide = source[...].astype(F32).reshape(groups, units, inputs, n_lanes)
         for u in range(units):
-            place(far[u * groups * inputs : (u + 1) * groups * inputs, :], 1, u)
-        wide = small[...].astype(F32).reshape(groups, 4, inputs, n_lanes)
-        for origin in range(4):
-            place(wide[:, origin].reshape(groups * inputs, n_lanes).astype(BF16), origin, units)
-        own = right[pl.ds(pl.multiple_of(where[0] * n_rows, n_rows), n_rows), :]
-        left[0:n_rows, :] = own
-        lane = lax.broadcasted_iota(jnp.int32, (n_rows, n_lanes), 1)
-        for s in range(right.shape[1] // n_lanes):
-            lanes = slice(s * n_lanes, (s + 1) * n_lanes)
-            swapped = pltpu.roll(own[:, lanes].astype(F32), UNIT, 1)
-            left[n_rows:, lanes] = jnp.where(lane < UNIT, swapped, -swapped).astype(BF16)
-
-    at = pl.multiple_of(pl.program_id(0) * COLUMNS, COLUMNS)
-    product = lax.dot_general(
-        left[...],
-        right[pl.ds(at, COLUMNS), :],
-        (((1,), (1,)), ((), ())),
-        preferred_element_type=F32,
-    )
+            place(wide[:, u].reshape(groups * inputs, n_lanes).astype(BF16), origin, u)
+    for u in range(units):
+        place(far[u * groups * inputs : (u + 1) * groups * inputs, :], 1, u)
+    wide = small[...].astype(F32).reshape(groups, 4, inputs, n_lanes)
+    for origin in range(4):
+        place(wide[:, origin].reshape(groups * inputs, n_lanes).astype(BF16), origin, units)
+    own = pl.ds(pl.multiple_of(where[0] * n_rows, n_rows), n_rows)
+    lane = lax.broadcasted_iota(jnp.int32, (n_rows, n_lanes), 1)
+    copies = []
     for part in range(2):
-        out[part, 0] = product[part * n_rows : (part + 1) * n_rows] * scale
+        if part == 1:
+            for s in range(right.shape[1] // n_lanes):
+                lanes = slice(s * n_lanes, (s + 1) * n_lanes)
+                swapped = pltpu.roll(right[own, lanes].astype(F32), UNIT, 1)
+                left[:, lanes] = jnp.where(lane < UNIT, swapped, -swapped).astype(BF16)
+        for block in range(right.shape[0] // COLUMNS):
+            columns = slice(block * COLUMNS, (block + 1) * COLUMNS)
+            product = lax.dot_general(
+                left[...] if part else right[own, :],
+                right[columns, :],
+                (((1,), (1,)), ((), ())),
+                preferred_element_type=F32,
+            )
+            ready[block, part] = product * scale
+            copies.append(
+                pltpu.make_async_copy(
+                    ready.at[block, part], out.at[part, 0, :, columns], sem.at[block, part]
+                )
+            )
+            copies[-1].start()
+    for copy in copies:
+        copy.wait()
 
 
 def visibilities(where, sources, inputs, scale):
@@ -225,15 +232,15 @@
     length = 2 * (depth // inputs + 1) * lanes
     return pl.pallas_call(
         functools.partial(visibility_kernel, inputs, scale),
-        grid_spec=pltpu.PrefetchScalarGridSpec(
-            num_scalar_prefetch=1,
-            grid=(total // COLUMNS,),
-            in_specs=[
-                pl.BlockSpec(source.shape, lambda r, w, n=source.ndim: (0,) * n) for source in sources
-            ],
-            out_specs=pl.BlockSpec((2, 1, total // 2, COLUMNS), lambda r, w: (0, 0, 0, r)),
-            scratch_shapes=[pltpu.VMEM((total, length), BF16), pltpu.VMEM((total, length), BF16)],
-        ),
+        in_specs=[pl.BlockSpec(memory_space=pltpu.SMEM)]
+        + [pl.BlockSpec(memory_space=pltpu.VMEM)] * len(sources),
+        out_specs=pl.BlockSpec(memory_space=pl.ANY),
+        scratch_shapes=[
+            pltpu.VMEM((total, length), BF16),
+            pltpu.VMEM((total // 2, length), BF16),
+            pltpu.VMEM((total // COLUMNS, 2, total // 2, COLUMNS), F32),
+            pltpu.SemaphoreType.DMA((total // COLUMNS, 2)),
+        ],
         out_shape=jax.ShapeDtypeStruct((2, 1, total // 2, total), F32),
         compiler_params=pltpu.CompilerParams(vmem_limit_bytes=VMEM_VIS),
         cost_estimate=pl.CostEstimate(

time: 79.3 us -> 78.2 us (0.986)
  Pallas kernels: 19.7 us -> 18.5 us
    pallas_call x1, Pallas kernels: 5.57 us -> 4.45 us  [visibilities(): pl.pallas_call(functools.partial(visibility_kernel, inputs, scale), in_sp...]
where the time goes in v7:
time: 78.2 us; the launch traced here: 77.9 us
  waiting for transfers between devices  29.2 us (37%)
  starting transfers between devices  27.3 us (35%)
  Pallas kernels  18.5 us (24%)
  other arithmetic  1.63 us (2%)
  local copies, waits for them, and re-layouts  1.11 us (1%)
    all_to_all x2, starting transfers between devices, over_plane(): return lax.all_to_all(array, PLANE, split_axis=0, concat_axis=0, tiled=True)  19.1 us
    ppermute x6, waiting for transfers between devices, swap(): return lax.ppermute(array, ('ta', 'xh'), route)  16.3 us
    pallas_call x2, Pallas kernels, filterbank(): pl.pallas_call(functools.partial(filterbank_kernel, first, halo_at), in_s...  14 us
    all_to_all x2, waiting for transfers between devices, over_plane(): return lax.all_to_all(array, PLANE, split_axis=0, concat_axis=0, tiled=True)  12.9 us
    ppermute x6, starting transfers between devices, swap(): return lax.ppermute(array, ('ta', 'xh'), route)  6.11 us
    pallas_call x1, Pallas kernels, visibilities(): pl.pallas_call(functools.partial(visibility_kernel, inputs, scale), in_sp...  4.45 us
    ppermute x1, starting transfers between devices, local(): lax.ppermute(last, 'ta', [(i, (i + 1) % n_time) for i in range(n_time)])  2.13 us
  transfers between devices with their start and end apart: 9, of which 7 were waited for; matrix products, arithmetic and copies ran while one was open for 3% of the time, Pallas kernels for 6%

profile of v7, /device:TPU:1, one launch (start us, length us, event | category | flops | bytes accessed | tf_op | source)
XLA Modules:
  0.0 77.9 jit_solution(1392317588168162734)
XLA Ops:
  0.0 9.3 %shard_map.46 = (bf16[128,24,128]{2,1,0:T(8,128)(2,1)}, bf16[4,8,2048]{2,1,0:T(8,128)(2,1)}) custom-call(bf16[256,8,2048]{2,1,0:T(8,128)(2,1)} %bitcast.17, bf16[256,8,2048]{2,1,0:T(8,128)(2,1)} %bitcast.18, f32[4,2048]{1,0:T(4,128)} %constant.37.clone.window, bf16[2048,256]{1,0:T(8,128)(2,1)} %constant.39.clone.table), custom_call_target="tpu_custom_call" | custom-call | flops 21474836480 | bytes 7340032 | tf_op jit(solution)/shard_map/pallas_call | solution.py:129
  9.3 2.1 %collective-permute-start = (bf16[4,8,2048]{2,1,0:T(8,128)(2,1)}, bf16[4,8,2048]{2,1,0:T(8,128)(2,1)S(1)}, u32[]{:S(2)}, u32[]{:S(2)}) collective-permute-start(bf16[4,8,2048]{2,1,0:T(8,128)(2,1)} %get-tuple-element.10), channel_id=1, source_target_pairs={{0,128},{128,0},{1,129},{129,1},{2,130},{130,2},{3,131},{131,3},{4... | collective-permute-start | bytes 393224 | tf_op jit(solution)/shard_map/ppermute | solution.py:290
  11.4 12.6 %all-to-all-start = ((bf16[64,2,24,128]{3,2,1,0:T(8,128)(2,1)}), bf16[64,2,24,128]{3,2,1,0:T(8,128)(2,1)S(1)}, u32[]{:S(2)}, u32[]{:S(2)}) async-start(bf16[64,2,24,128]{3,2,1,0:T(8,128)(2,1)} %bitcast.15), calls=%async_computation | async-start | bytes 1572864 | tf_op jit(solution)/shard_map/all_to_all | solution.py:265
  24.0 0.7 broadcast_select_fusion.halo
  24.7 4.7 %shard_map.47 = bf16[128,8,128]{2,1,0:T(8,128)(2,1)} custom-call(bf16[256,8,2048]{2,1,0:T(8,128)(2,1)} %bitcast.19, bf16[4,8,2048]{2,1,0:T(8,128)(2,1)} %broadcast_select_fusion.halo, f32[4,2048]{1,0:T(4,128)} %constant.37.clone.window, bf16[2048,256]{1,0:T(8,128)(2,1)} %constant.38.clone.table), custom_call_target="tpu_custom_call" | custom-call | flops 21474836480 | bytes 3145728 | tf_op jit(solution)/shard_map/pallas_call | solution.py:129
  29.5 1.0 %dynamic-slice_bitcast_fusion.3 = (bf16[64,8,128]{2,1,0:T(8,128)(2,1)S(1)}, bf16[64,8,128]{2,1,0:T(8,128)(2,1)S(1)}) fusion(bf16[2,64,8,128]{3,2,1,0:T(8,128)(2,1)} %bitcast.16, s32[]{:T(128)S(6)} %select_n.20, s32[]{:T(128)S(6)} %select_n.21), kind=kLoop, calls=%fused_computation.4 | loop fusion | bytes 524296 | tf_op jit(solution)/shard_map/jit(dynamic_index_in_dim)/squeeze | solution.py:270
  30.5 0.3 collective-permute-start.2
  30.8 2.5 %collective-permute-start.3 = (bf16[64,8,128]{2,1,0:T(8,128)(2,1)S(1)}, bf16[64,8,128]{2,1,0:T(8,128)(2,1)S(1)}, u32[]{:S(2)}, u32[]{:S(2)}) collective-permute-start(bf16[64,8,128]{2,1,0:T(8,128)(2,1)S(1)} %get-tuple-element.16), channel_id=1, source_target_pairs={{0,144},{16,128},{128,16},{144,0},{1,145},{17,129},{129,17},{145,1... | collective-permute-start | bytes 393224 | tf_op jit(solution)/shard_map/ppermute | solution.py:254
  33.3 0.5 collective-permute-start.1
  33.8 1.4 %collective-permute-done.2 = bf16[64,8,128]{2,1,0:T(8,128)(2,1)S(1)} collective-permute-done((bf16[64,8,128]{2,1,0:T(8,128)(2,1)S(1)}, bf16[64,8,128]{2,1,0:T(8,128)(2,1)S(1)}, u32[]{:S(2)}, u32[]{:S(2)}) %collective-permute-start.2) | collective-permute-done | bytes 131104 | tf_op jit(solution)/shard_map/ppermute | solution.py:254
  35.2 3.2 %collective-permute-done.3 = bf16[64,8,128]{2,1,0:T(8,128)(2,1)S(1)} collective-permute-done((bf16[64,8,128]{2,1,0:T(8,128)(2,1)S(1)}, bf16[64,8,128]{2,1,0:T(8,128)(2,1)S(1)}, u32[]{:S(2)}, u32[]{:S(2)}) %collective-permute-start.3) | collective-permute-done | bytes 131104 | tf_op jit(solution)/shard_map/ppermute | solution.py:254
  38.4 0.6 collective-permute-done.1
  39.0 0.9 %pad_maximum_fusion = bf16[64,32,128]{2,1,0:T(8,128)(2,1)} fusion(bf16[64,8,128]{2,1,0:T(8,128)(2,1)S(1)} %collective-permute-done.3, bf16[64,8,128]{2,1,0:T(8,128)(2,1)S(1)} %collective-permute-done.2, bf16[64,8,128]{2,1,0:T(8,128)(2,1)S(1)} %collective-permute-done.1, bf16[64,8,128]{2,1,0:T(8,128)(2,1)S(1)} %get-tuple-element.15), kind=kLoop, calls=%fused_computation | loop fusion | flops 2097152 | bytes 1048576 | tf_op jit(solution)/shard_map/concatenate | solution.py:294
  39.9 7.1 %all-to-all-done = bf16[64,2,24,128]{3,2,1,0:T(8,128)(2,1)S(1)} async-done(((bf16[64,2,24,128]{3,2,1,0:T(8,128)(2,1)}), bf16[64,2,24,128]{3,2,1,0:T(8,128)(2,1)S(1)}, u32[]{:S(2)}, u32[]{:S(2)}) %all-to-all-start) | async-done | bytes 786464 | tf_op jit(solution)/shard_map/all_to_all | solution.py:265
  47.0 0.1 dynamic-slice_bitcast_fusion
  47.1 2.5 %collective-permute-start.4 = (bf16[64,24,128]{2,1,0:T(8,128)(2,1)S(1)}, bf16[64,24,128]{2,1,0:T(8,128)(2,1)S(1)}, u32[]{:S(2)}, u32[]{:S(2)}) collective-permute-start(bf16[64,24,128]{2,1,0:T(8,128)(2,1)S(1)} %get-tuple-element.13), channel_id=1, source_target_pairs={{0,16},{16,0},{128,144},{144,128},{1,17},{17,1},{129,145},{145,129... | collective-permute-start | bytes 1179656 | tf_op jit(solution)/shard_map/ppermute | solution.py:254
  49.6 6.5 %all-to-all-start.1 = ((bf16[64,32,128]{2,1,0:T(8,128)(2,1)}), bf16[64,32,128]{2,1,0:T(8,128)(2,1)S(1)}, u32[]{:S(2)}, u32[]{:S(2)}) async-start(bf16[64,32,128]{2,1,0:T(8,128)(2,1)} %pad_maximum_fusion), calls=%async_computation.1 | async-start | bytes 1048576 | tf_op jit(solution)/shard_map/all_to_all | solution.py:265
  56.1 0.1 pad_add_fusion.where
  56.2 0.3 collective-permute-start.6
  56.5 2.6 %collective-permute-done.4.source = bf16[64,24,128]{2,1,0:T(8,128)(2,1)S(1)} collective-permute-done((bf16[64,24,128]{2,1,0:T(8,128)(2,1)S(1)}, bf16[64,24,128]{2,1,0:T(8,128)(2,1)S(1)}, u32[]{:S(2)}, u32[]{:S(2)}) %collective-permute-start.4) | collective-permute-done | bytes 393248 | tf_op jit(solution)/shard_map/ppermute | solution.py:254
  59.0 0.1 shard_map.48.far
  59.1 8.6 %collective-permute-done.6.both = bf16[64,24,128]{2,1,0:T(8,128)(2,1)S(1)} collective-permute-done((bf16[64,24,128]{2,1,0:T(8,128)(2,1)S(1)}, bf16[64,24,128]{2,1,0:T(8,128)(2,1)S(1)}, u32[]{:S(2)}, u32[]{:S(2)}) %collective-permute-start.6) | collective-permute-done | bytes 393248 | tf_op jit(solution)/shard_map/ppermute | solution.py:254
  67.7 5.8 %all-to-all-done.1.small = bf16[64,32,128]{2,1,0:T(8,128)(2,1)S(1)} async-done(((bf16[64,32,128]{2,1,0:T(8,128)(2,1)}), bf16[64,32,128]{2,1,0:T(8,128)(2,1)S(1)}, u32[]{:S(2)}, u32[]{:S(2)}) %all-to-all-start.1) | async-done | bytes 524320 | tf_op jit(solution)/shard_map/all_to_all | solution.py:265
  73.4 4.5 %shard_map.49 = f32[2,1,512,1024]{3,2,1,0:T(8,128)} custom-call(s32[2]{0:T(128)S(1)} %pad_add_fusion.where, bf16[64,24,128]{2,1,0:T(8,128)(2,1)S(1)} %get-tuple-element.14.mine, bf16[1536,128]{1,0:T(8,128)(2,1)S(1)} %shard_map.48.far, bf16[64,24,128]{2,1,0:T(8,128)(2,1)S(1)} %collective-permute-done.5.near, ...), custom_call_target="tpu_custom_call" | custom-call | flops 2147483648 | bytes 7340032 | tf_op jit(solution)/shard_map/pallas_call | solution.py:233
  (3 shorter events, 0.0 us)
Async XLA Ops:
  9.3 14.8 %collective-permute-start = (bf16[4,8,2048]{2,1,0:T(8,128)(2,1)}, bf16[4,8,2048]{2,1,0:T(8,128)(2,1)S(1)}, u32[]{:S(2)}, u32[]{:S(2)}) collective-permute-start(bf16[4,8,2048]{2,1,0:T(8,128)(2,1)} %get-tuple-element.10), channel_id=1, source_target_pairs={{0,128},{128,0},{1,129},{129,1},{2,130},{130,2},{3,131},{131,3},{4... | collective-permute-start | bytes 393224 | tf_op jit(solution)/shard_map/ppermute | solution.py:290
  11.4 35.6 %all-to-all-start = ((bf16[64,2,24,128]{3,2,1,0:T(8,128)(2,1)}), bf16[64,2,24,128]{3,2,1,0:T(8,128)(2,1)S(1)}, u32[]{:S(2)}, u32[]{:S(2)}) async-start(bf16[64,2,24,128]{3,2,1,0:T(8,128)(2,1)} %bitcast.15), calls=%async_computation | async-start | bytes 1572864 | tf_op jit(solution)/shard_map/all_to_all | solution.py:265
  30.5 4.7 %collective-permute-start.2 = (bf16[64,8,128]{2,1,0:T(8,128)(2,1)S(1)}, bf16[64,8,128]{2,1,0:T(8,128)(2,1)S(1)}, u32[]{:S(2)}, u32[]{:S(2)}) collective-permute-start(bf16[64,8,128]{2,1,0:T(8,128)(2,1)S(1)} %get-tuple-element.15), channel_id=1, source_target_pairs={{0,128},{16,144},{128,0},{144,16},{1,129},{17,145},{129,1},{145,17... | collective-permute-start | bytes 393224 | tf_op jit(solution)/shard_map/ppermute | solution.py:254
  30.8 7.6 %collective-permute-start.3 = (bf16[64,8,128]{2,1,0:T(8,128)(2,1)S(1)}, bf16[64,8,128]{2,1,0:T(8,128)(2,1)S(1)}, u32[]{:S(2)}, u32[]{:S(2)}) collective-permute-start(bf16[64,8,128]{2,1,0:T(8,128)(2,1)S(1)} %get-tuple-element.16), channel_id=1, source_target_pairs={{0,144},{16,128},{128,16},{144,0},{1,145},{17,129},{129,17},{145,1... | collective-permute-start | bytes 393224 | tf_op jit(solution)/shard_map/ppermute | solution.py:254
  33.3 5.7 %collective-permute-start.1 = (bf16[64,8,128]{2,1,0:T(8,128)(2,1)S(1)}, bf16[64,8,128]{2,1,0:T(8,128)(2,1)S(1)}, u32[]{:S(2)}, u32[]{:S(2)}) collective-permute-start(bf16[64,8,128]{2,1,0:T(8,128)(2,1)S(1)} %get-tuple-element.16), channel_id=1, source_target_pairs={{0,16},{16,0},{128,144},{144,128},{1,17},{17,1},{129,145},{145,129... | collective-permute-start | bytes 393224 | tf_op jit(solution)/shard_map/ppermute | solution.py:254
  47.1 11.9 %collective-permute-start.4 = (bf16[64,24,128]{2,1,0:T(8,128)(2,1)S(1)}, bf16[64,24,128]{2,1,0:T(8,128)(2,1)S(1)}, u32[]{:S(2)}, u32[]{:S(2)}) collective-permute-start(bf16[64,24,128]{2,1,0:T(8,128)(2,1)S(1)} %get-tuple-element.13), channel_id=1, source_target_pairs={{0,16},{16,0},{128,144},{144,128},{1,17},{17,1},{129,145},{145,129... | collective-permute-start | bytes 1179656 | tf_op jit(solution)/shard_map/ppermute | solution.py:254
  49.6 23.8 %all-to-all-start.1 = ((bf16[64,32,128]{2,1,0:T(8,128)(2,1)}), bf16[64,32,128]{2,1,0:T(8,128)(2,1)S(1)}, u32[]{:S(2)}, u32[]{:S(2)}) async-start(bf16[64,32,128]{2,1,0:T(8,128)(2,1)} %pad_maximum_fusion), calls=%async_computation.1 | async-start | bytes 1048576 | tf_op jit(solution)/shard_map/all_to_all | solution.py:265
  56.2 11.5 %collective-permute-start.6 = (bf16[64,24,128]{2,1,0:T(8,128)(2,1)S(1)}, bf16[64,24,128]{2,1,0:T(8,128)(2,1)S(1)}, u32[]{:S(2)}, u32[]{:S(2)}) collective-permute-start(bf16[64,24,128]{2,1,0:T(8,128)(2,1)S(1)} %get-tuple-element.13), channel_id=1, source_target_pairs={{0,144},{16,128},{128,16},{144,0},{1,145},{17,129},{129,17},{145,1... | collective-permute-start | bytes 1179656 | tf_op jit(solution)/shard_map/ppermute | solution.py:254
  56.5 11.2 %collective-permute-start.5 = (bf16[64,24,128]{2,1,0:T(8,128)(2,1)S(1)}, bf16[64,24,128]{2,1,0:T(8,128)(2,1)S(1)}, u32[]{:S(2)}, u32[]{:S(2)}) collective-permute-start(bf16[64,24,128]{2,1,0:T(8,128)(2,1)S(1)} %get-tuple-element.14.mine), channel_id=1, source_target_pairs={{0,128},{16,144},{128,0},{144,16},{1,129},{17,145},{129,1},{145,17... | collective-permute-start | bytes 1179656 | tf_op jit(solution)/shard_map/ppermute | solution.py:254

commit v8 on v7

--- a/solution.py
+++ b/solution.py
@@ -45,10 +45,10 @@
 
 
 def filterbank_kernel(first, halo_at, frames, halo, window, table, *refs):
-    out, (held, weight, dft, summed, turned, sem) = refs[0], refs[-6:]
+    out, (held, weight, dft, summed, turned, ready, sem) = refs[0], refs[-7:]
     inputs = held.shape[1]
-    count = out.shape[0]
-    units = out.shape[1] // inputs
+    count, depth = ready.shape[:2]
+    units = depth // inputs
     span = PIECE * inputs
     pieces = UNIT // PIECE
 
@@ -115,9 +115,21 @@
     lax.fori_loop(0, units * pieces, body, 0)
     for i in range(inputs):
         turn(units - 1, i)
-    out[...] = turned[...].reshape(count, units * inputs, 2 * UNIT).astype(BF16)
-    for last in refs[1:-6]:
-        last[...] = held[units * UNIT :]
+    copies = [
+        pltpu.make_async_copy(held.at[pl.ds(units * UNIT, HALO)], last, sem.at[0])
+        for last in refs[1:-7]
+    ]
+    for copy_out in copies:
+        copy_out.start()
+    share = count // 4
+    for quarter in range(4):
+        some = turned[quarter * share * units * inputs : (quarter + 1) * share * units * inputs, :]
+        here = pl.ds(quarter * share, share)
+        ready[here] = some.reshape(share, units * inputs, 2 * UNIT).astype(BF16)
+        copies.append(pltpu.make_async_copy(ready.at[here], out.at[here], sem.at[3 + quarter]))
+        copies[-1].start()
+    for copy_out in copies:
+        copy_out.wait()
 
 
 def filterbank(frames, first, spectra, halo, halo_at, window, table, tail):
@@ -125,11 +137,10 @@
     count = table.shape[1] // 2
     units = spectra // UNIT
     there = pl.BlockSpec(memory_space=pl.ANY)
-    here = pl.BlockSpec(memory_space=pltpu.VMEM)
     return pl.pallas_call(
         functools.partial(filterbank_kernel, first, halo_at),
         in_specs=[there] * 4,
-        out_specs=[here] * (1 + tail),
+        out_specs=[there] * (1 + tail),
         out_shape=[
             jax.ShapeDtypeStruct((count, units * inputs, 2 * UNIT), BF16),
             jax.ShapeDtypeStruct((HALO, inputs, FRAME), BF16),
@@ -140,7 +151,8 @@
             pltpu.VMEM(table.shape, BF16),
             pltpu.VMEM((2, 2, UNIT * inputs, count), F32),
             pltpu.VMEM((count * units * inputs, 2 * UNIT), F32),
-            pltpu.SemaphoreType.DMA((3 + spectra // PIECE,)),
+            pltpu.VMEM((count, units * inputs, 2 * UNIT), BF16),
+            pltpu.SemaphoreType.DMA((3 + max(4, spectra // PIECE),)),
         ],
         compiler_params=pltpu.CompilerParams(vmem_limit_bytes=VMEM_BANK),
         cost_estimate=pl.CostEstimate(

time: 78.2 us -> 78.1 us (level)
  no operation moved by 1% of the time
where the time goes in v8:
time: 78.1 us; the launch traced here: 77.8 us
  waiting for transfers between devices  29.2 us (37%)
  starting transfers between devices  27.3 us (35%)
  Pallas kernels  18.5 us (24%)
  other arithmetic  1.63 us (2%)
  local copies, waits for them, and re-layouts  1.11 us (1%)
    all_to_all x2, starting transfers between devices, over_plane(): return lax.all_to_all(array, PLANE, split_axis=0, concat_axis=0, tiled=True)  19.1 us
    ppermute x6, waiting for transfers between devices, swap(): return lax.ppermute(array, ('ta', 'xh'), route)  16.3 us
    pallas_call x2, Pallas kernels, filterbank(): pl.pallas_call(functools.partial(filterbank_kernel, first, halo_at), in_s...  13.9 us
    all_to_all x2, waiting for transfers between devices, over_plane(): return lax.all_to_all(array, PLANE, split_axis=0, concat_axis=0, tiled=True)  12.9 us
    ppermute x6, starting transfers between devices, swap(): return lax.ppermute(array, ('ta', 'xh'), route)  6.1 us
    pallas_call x1, Pallas kernels, visibilities(): pl.pallas_call(functools.partial(visibility_kernel, inputs, scale), in_sp...  4.45 us
    ppermute x1, starting transfers between devices, local(): lax.ppermute(last, 'ta', [(i, (i + 1) % n_time) for i in range(n_time)])  2.13 us
  transfers between devices with their start and end apart: 9, of which 7 were waited for; matrix products, arithmetic and copies ran while one was open for 3% of the time, Pallas kernels for 6%

profile of v8, /device:TPU:1, one launch (start us, length us, event | category | flops | bytes accessed | tf_op | source)
XLA Modules:
  0.0 77.8 jit_solution(9115485961722488264)
XLA Ops:
  0.0 9.2 %shard_map.46 = (bf16[128,24,128]{2,1,0:T(8,128)(2,1)}, bf16[4,8,2048]{2,1,0:T(8,128)(2,1)}) custom-call(bf16[256,8,2048]{2,1,0:T(8,128)(2,1)} %bitcast.17, bf16[256,8,2048]{2,1,0:T(8,128)(2,1)} %bitcast.18, f32[4,2048]{1,0:T(4,128)} %constant.37.clone.window, bf16[2048,256]{1,0:T(8,128)(2,1)} %constant.39.clone.table), custom_call_target="tpu_custom_call" | custom-call | flops 21474836480 | bytes 7340032 | tf_op jit(solution)/shard_map/pallas_call | solution.py:140
  9.2 2.1 %collective-permute-start = (bf16[4,8,2048]{2,1,0:T(8,128)(2,1)}, bf16[4,8,2048]{2,1,0:T(8,128)(2,1)S(1)}, u32[]{:S(2)}, u32[]{:S(2)}) collective-permute-start(bf16[4,8,2048]{2,1,0:T(8,128)(2,1)} %get-tuple-element.10), channel_id=1, source_target_pairs={{0,128},{128,0},{1,129},{129,1},{2,130},{130,2},{3,131},{131,3},{4... | collective-permute-start | bytes 393224 | tf_op jit(solution)/shard_map/ppermute | solution.py:302
  11.4 12.6 %all-to-all-start = ((bf16[64,2,24,128]{3,2,1,0:T(8,128)(2,1)}), bf16[64,2,24,128]{3,2,1,0:T(8,128)(2,1)S(1)}, u32[]{:S(2)}, u32[]{:S(2)}) async-start(bf16[64,2,24,128]{3,2,1,0:T(8,128)(2,1)} %bitcast.15), calls=%async_computation | async-start | bytes 1572864 | tf_op jit(solution)/shard_map/all_to_all | solution.py:277
  24.0 0.7 broadcast_select_fusion.halo
  24.7 4.7 %shard_map.47 = bf16[128,8,128]{2,1,0:T(8,128)(2,1)} custom-call(bf16[256,8,2048]{2,1,0:T(8,128)(2,1)} %bitcast.19, bf16[4,8,2048]{2,1,0:T(8,128)(2,1)} %broadcast_select_fusion.halo, f32[4,2048]{1,0:T(4,128)} %constant.37.clone.window, bf16[2048,256]{1,0:T(8,128)(2,1)} %constant.38.clone.table), custom_call_target="tpu_custom_call" | custom-call | flops 21474836480 | bytes 3145728 | tf_op jit(solution)/shard_map/pallas_call | solution.py:140
  29.4 1.0 %dynamic-slice_bitcast_fusion.3 = (bf16[64,8,128]{2,1,0:T(8,128)(2,1)S(1)}, bf16[64,8,128]{2,1,0:T(8,128)(2,1)S(1)}) fusion(bf16[2,64,8,128]{3,2,1,0:T(8,128)(2,1)} %bitcast.16, s32[]{:T(128)S(6)} %select_n.20, s32[]{:T(128)S(6)} %select_n.21), kind=kLoop, calls=%fused_computation.4 | loop fusion | bytes 524296 | tf_op jit(solution)/shard_map/jit(dynamic_index_in_dim)/squeeze | solution.py:282
  30.4 0.3 collective-permute-start.2
  30.7 2.5 %collective-permute-start.3 = (bf16[64,8,128]{2,1,0:T(8,128)(2,1)S(1)}, bf16[64,8,128]{2,1,0:T(8,128)(2,1)S(1)}, u32[]{:S(2)}, u32[]{:S(2)}) collective-permute-start(bf16[64,8,128]{2,1,0:T(8,128)(2,1)S(1)} %get-tuple-element.16), channel_id=1, source_target_pairs={{0,144},{16,128},{128,16},{144,0},{1,145},{17,129},{129,17},{145,1... | collective-permute-start | bytes 393224 | tf_op jit(solution)/shard_map/ppermute | solution.py:266
  33.2 0.5 collective-permute-start.1
  33.7 1.4 %collective-permute-done.2 = bf16[64,8,128]{2,1,0:T(8,128)(2,1)S(1)} collective-permute-done((bf16[64,8,128]{2,1,0:T(8,128)(2,1)S(1)}, bf16[64,8,128]{2,1,0:T(8,128)(2,1)S(1)}, u32[]{:S(2)}, u32[]{:S(2)}) %collective-permute-start.2) | collective-permute-done | bytes 131104 | tf_op jit(solution)/shard_map/ppermute | solution.py:266
  35.1 3.2 %collective-permute-done.3 = bf16[64,8,128]{2,1,0:T(8,128)(2,1)S(1)} collective-permute-done((bf16[64,8,128]{2,1,0:T(8,128)(2,1)S(1)}, bf16[64,8,128]{2,1,0:T(8,128)(2,1)S(1)}, u32[]{:S(2)}, u32[]{:S(2)}) %collective-permute-start.3) | collective-permute-done | bytes 131104 | tf_op jit(solution)/shard_map/ppermute | solution.py:266
  38.3 0.6 collective-permute-done.1
  38.9 0.9 %pad_maximum_fusion = bf16[64,32,128]{2,1,0:T(8,128)(2,1)} fusion(bf16[64,8,128]{2,1,0:T(8,128)(2,1)S(1)} %collective-permute-done.3, bf16[64,8,128]{2,1,0:T(8,128)(2,1)S(1)} %collective-permute-done.2, bf16[64,8,128]{2,1,0:T(8,128)(2,1)S(1)} %collective-permute-done.1, bf16[64,8,128]{2,1,0:T(8,128)(2,1)S(1)} %get-tuple-element.15), kind=kLoop, calls=%fused_computation | loop fusion | flops 2097152 | bytes 1048576 | tf_op jit(solution)/shard_map/concatenate | solution.py:306
  39.8 7.1 %all-to-all-done = bf16[64,2,24,128]{3,2,1,0:T(8,128)(2,1)S(1)} async-done(((bf16[64,2,24,128]{3,2,1,0:T(8,128)(2,1)}), bf16[64,2,24,128]{3,2,1,0:T(8,128)(2,1)S(1)}, u32[]{:S(2)}, u32[]{:S(2)}) %all-to-all-start) | async-done | bytes 786464 | tf_op jit(solution)/shard_map/all_to_all | solution.py:277
  47.0 0.1 dynamic-slice_bitcast_fusion
  47.1 2.5 %collective-permute-start.4 = (bf16[64,24,128]{2,1,0:T(8,128)(2,1)S(1)}, bf16[64,24,128]{2,1,0:T(8,128)(2,1)S(1)}, u32[]{:S(2)}, u32[]{:S(2)}) collective-permute-start(bf16[64,24,128]{2,1,0:T(8,128)(2,1)S(1)} %get-tuple-element.13), channel_id=1, source_target_pairs={{0,16},{16,0},{128,144},{144,128},{1,17},{17,1},{129,145},{145,129... | collective-permute-start | bytes 1179656 | tf_op jit(solution)/shard_map/ppermute | solution.py:266
  49.6 6.5 %all-to-all-start.1 = ((bf16[64,32,128]{2,1,0:T(8,128)(2,1)}), bf16[64,32,128]{2,1,0:T(8,128)(2,1)S(1)}, u32[]{:S(2)}, u32[]{:S(2)}) async-start(bf16[64,32,128]{2,1,0:T(8,128)(2,1)} %pad_maximum_fusion), calls=%async_computation.1 | async-start | bytes 1048576 | tf_op jit(solution)/shard_map/all_to_all | solution.py:277
  56.1 0.1 pad_add_fusion.where
  56.1 0.3 collective-permute-start.6
  56.4 2.6 %collective-permute-done.4.source = bf16[64,24,128]{2,1,0:T(8,128)(2,1)S(1)} collective-permute-done((bf16[64,24,128]{2,1,0:T(8,128)(2,1)S(1)}, bf16[64,24,128]{2,1,0:T(8,128)(2,1)S(1)}, u32[]{:S(2)}, u32[]{:S(2)}) %collective-permute-start.4) | collective-permute-done | bytes 393248 | tf_op jit(solution)/shard_map/ppermute | solution.py:266
  59.0 0.1 shard_map.48.far
  59.0 8.6 %collective-permute-done.6.both = bf16[64,24,128]{2,1,0:T(8,128)(2,1)S(1)} collective-permute-done((bf16[64,24,128]{2,1,0:T(8,128)(2,1)S(1)}, bf16[64,24,128]{2,1,0:T(8,128)(2,1)S(1)}, u32[]{:S(2)}, u32[]{:S(2)}) %collective-permute-start.6) | collective-permute-done | bytes 393248 | tf_op jit(solution)/shard_map/ppermute | solution.py:266
  67.6 5.8 %all-to-all-done.1.small = bf16[64,32,128]{2,1,0:T(8,128)(2,1)S(1)} async-done(((bf16[64,32,128]{2,1,0:T(8,128)(2,1)}), bf16[64,32,128]{2,1,0:T(8,128)(2,1)S(1)}, u32[]{:S(2)}, u32[]{:S(2)}) %all-to-all-start.1) | async-done | bytes 524320 | tf_op jit(solution)/shard_map/all_to_all | solution.py:277
  73.4 4.5 %shard_map.49 = f32[2,1,512,1024]{3,2,1,0:T(8,128)} custom-call(s32[2]{0:T(128)S(1)} %pad_add_fusion.where, bf16[64,24,128]{2,1,0:T(8,128)(2,1)S(1)} %get-tuple-element.14.mine, bf16[1536,128]{1,0:T(8,128)(2,1)S(1)} %shard_map.48.far, bf16[64,24,128]{2,1,0:T(8,128)(2,1)S(1)} %collective-permute-done.5.near, ...), custom_call_target="tpu_custom_call" | custom-call | flops 2147483648 | bytes 7340032 | tf_op jit(solution)/shard_map/pallas_call | solution.py:245
  (3 shorter events, 0.0 us)
Async XLA Ops:
  9.2 14.8 %collective-permute-start = (bf16[4,8,2048]{2,1,0:T(8,128)(2,1)}, bf16[4,8,2048]{2,1,0:T(8,128)(2,1)S(1)}, u32[]{:S(2)}, u32[]{:S(2)}) collective-permute-start(bf16[4,8,2048]{2,1,0:T(8,128)(2,1)} %get-tuple-element.10), channel_id=1, source_target_pairs={{0,128},{128,0},{1,129},{129,1},{2,130},{130,2},{3,131},{131,3},{4... | collective-permute-start | bytes 393224 | tf_op jit(solution)/shard_map/ppermute | solution.py:302
  11.4 35.6 %all-to-all-start = ((bf16[64,2,24,128]{3,2,1,0:T(8,128)(2,1)}), bf16[64,2,24,128]{3,2,1,0:T(8,128)(2,1)S(1)}, u32[]{:S(2)}, u32[]{:S(2)}) async-start(bf16[64,2,24,128]{3,2,1,0:T(8,128)(2,1)} %bitcast.15), calls=%async_computation | async-start | bytes 1572864 | tf_op jit(solution)/shard_map/all_to_all | solution.py:277
  30.4 4.7 %collective-permute-start.2 = (bf16[64,8,128]{2,1,0:T(8,128)(2,1)S(1)}, bf16[64,8,128]{2,1,0:T(8,128)(2,1)S(1)}, u32[]{:S(2)}, u32[]{:S(2)}) collective-permute-start(bf16[64,8,128]{2,1,0:T(8,128)(2,1)S(1)} %get-tuple-element.15), channel_id=1, source_target_pairs={{0,128},{16,144},{128,0},{144,16},{1,129},{17,145},{129,1},{145,17... | collective-permute-start | bytes 393224 | tf_op jit(solution)/shard_map/ppermute | solution.py:266
  30.7 7.6 %collective-permute-start.3 = (bf16[64,8,128]{2,1,0:T(8,128)(2,1)S(1)}, bf16[64,8,128]{2,1,0:T(8,128)(2,1)S(1)}, u32[]{:S(2)}, u32[]{:S(2)}) collective-permute-start(bf16[64,8,128]{2,1,0:T(8,128)(2,1)S(1)} %get-tuple-element.16), channel_id=1, source_target_pairs={{0,144},{16,128},{128,16},{144,0},{1,145},{17,129},{129,17},{145,1... | collective-permute-start | bytes 393224 | tf_op jit(solution)/shard_map/ppermute | solution.py:266
  33.2 5.7 %collective-permute-start.1 = (bf16[64,8,128]{2,1,0:T(8,128)(2,1)S(1)}, bf16[64,8,128]{2,1,0:T(8,128)(2,1)S(1)}, u32[]{:S(2)}, u32[]{:S(2)}) collective-permute-start(bf16[64,8,128]{2,1,0:T(8,128)(2,1)S(1)} %get-tuple-element.16), channel_id=1, source_target_pairs={{0,16},{16,0},{128,144},{144,128},{1,17},{17,1},{129,145},{145,129... | collective-permute-start | bytes 393224 | tf_op jit(solution)/shard_map/ppermute | solution.py:266
  47.1 11.9 %collective-permute-start.4 = (bf16[64,24,128]{2,1,0:T(8,128)(2,1)S(1)}, bf16[64,24,128]{2,1,0:T(8,128)(2,1)S(1)}, u32[]{:S(2)}, u32[]{:S(2)}) collective-permute-start(bf16[64,24,128]{2,1,0:T(8,128)(2,1)S(1)} %get-tuple-element.13), channel_id=1, source_target_pairs={{0,16},{16,0},{128,144},{144,128},{1,17},{17,1},{129,145},{145,129... | collective-permute-start | bytes 1179656 | tf_op jit(solution)/shard_map/ppermute | solution.py:266
  49.6 23.8 %all-to-all-start.1 = ((bf16[64,32,128]{2,1,0:T(8,128)(2,1)}), bf16[64,32,128]{2,1,0:T(8,128)(2,1)S(1)}, u32[]{:S(2)}, u32[]{:S(2)}) async-start(bf16[64,32,128]{2,1,0:T(8,128)(2,1)} %pad_maximum_fusion), calls=%async_computation.1 | async-start | bytes 1048576 | tf_op jit(solution)/shard_map/all_to_all | solution.py:277
  56.1 11.5 %collective-permute-start.6 = (bf16[64,24,128]{2,1,0:T(8,128)(2,1)S(1)}, bf16[64,24,128]{2,1,0:T(8,128)(2,1)S(1)}, u32[]{:S(2)}, u32[]{:S(2)}) collective-permute-start(bf16[64,24,128]{2,1,0:T(8,128)(2,1)S(1)} %get-tuple-element.13), channel_id=1, source_target_pairs={{0,144},{16,128},{128,16},{144,0},{1,145},{17,129},{129,17},{145,1... | collective-permute-start | bytes 1179656 | tf_op jit(solution)/shard_map/ppermute | solution.py:266
  56.4 11.2 %collective-permute-start.5 = (bf16[64,24,128]{2,1,0:T(8,128)(2,1)S(1)}, bf16[64,24,128]{2,1,0:T(8,128)(2,1)S(1)}, u32[]{:S(2)}, u32[]{:S(2)}) collective-permute-start(bf16[64,24,128]{2,1,0:T(8,128)(2,1)S(1)} %get-tuple-element.14.mine), channel_id=1, source_target_pairs={{0,128},{16,144},{128,0},{144,16},{1,129},{17,145},{129,1},{145,17... | collective-permute-start | bytes 1179656 | tf_op jit(solution)/shard_map/ppermute | solution.py:266
